TPU v7x, 32 devices: a whole 2x2x4 slice. The times are simulated.
32 devices in a mesh: phase: 4 (over y, core), axial: 2 (over x), radial: 4 (over z).
Axes of the slice: x: 2, y: 2, z: 4, core: 2. Of those that a mesh axis runs over, the one named last changes fastest.
Arguments:
- psi_start: float32 [4, 10, 8, 64, 128], P('phase', None, 'axial', 'radial'), may hold values from -6 to 6
- source: float32 [4, 10, 8, 64, 128], P('phase', None, 'axial', 'radial'), may hold values from -6 to 6
- face_coef: bfloat16 [6, 8, 64, 128], P(None, 'axial', 'radial'), may hold values from 0.099609375 to 1
- diag_coef: float32 [8, 64, 128], P('axial', 'radial'), may hold values from 6 to 10
- flux_jac: float32 [6, 2, 5, 5], replicated, may hold values from -2 to 2
- omega: float32 [1], replicated, may hold values from 0.5 to 2
- metric: float32 [3, 10], replicated, may hold values from -2 to 2
- mode_shape: bfloat16 [12, 3, 8, 64, 128], P(None, None, 'axial', 'radial'), may hold values from -6 to 6
- phase_weight: float32 [4], P('phase'), may hold values from 0.05 to 0.5
- pairing: int32 [2, 4, 64], P('axial', 'radial'), may hold values from 0 to 63, each once within a row
- owner_order: int32 [2, 4, 8192], P('axial', 'radial'), may hold values from 0 to 8191, each once within a row
Outputs:
- psi_out: float32 [4, 10, 8, 64, 128], P('phase', None, 'axial', 'radial')
- sens: float32 [12, 2, 4, 8192], P(None, 'axial', 'radial', 'phase')
Inputs may be any that keep to these rules, and one draw needn't show every extreme that they name: `pairing`: each tile's row is a permutation of its pitch-end nodes. `owner_order`: each tile's row is a permutation of its cells.
All inputs are finite; a program needn't handle non-finite values.
Results may differ from a plain program's by a relative error of at most 0.0003.
Values sent between devices are 32-bit elements; how exact they have to be, the bound alone decides.
A program may use at most 64 MiB of HBM per device.

v0:
```python
import math

import jax
import jax.numpy as jnp
from jax import lax
from jax.sharding import PartitionSpec as P

BLADES = 16
ITERS = 4


RELAX = 0.8


def padded(value, sides, width):
    for axis, dim in sides:
        count, length = (lax.axis_size(axis), value.shape[dim])
        up = [(i, (i + 1) % count) for i in range(count - 1)]
        down = [(j, i) for i, j in up]
        last = lax.slice_in_dim(value, length - width, length, axis=dim)
        leading = lax.slice_in_dim(value, 0, width, axis=dim)
        before = lax.ppermute(last, axis, up)
        after = lax.ppermute(leading, axis, down)
        value = jnp.concatenate([before, value, after], axis=dim)
    return value


def build_matrices(flux_jac):
    real_part = jnp.swapaxes(flux_jac[:, 0], 1, 2)
    imag_part = jnp.swapaxes(flux_jac[:, 1], 1, 2)
    top_rows = jnp.concatenate([real_part, imag_part], axis=2)
    low_rows = jnp.concatenate([-imag_part, real_part], axis=2)
    return jnp.concatenate([top_rows, low_rows], axis=1)


def rotate(values, angle):
    shape = (-1,) + (1,) * (values.ndim - 1)
    cosine = jnp.cos(angle).reshape(shape)
    sine = jnp.sin(angle).reshape(shape)
    half = values.shape[1] // 2
    real_part = values[:, :half]
    imag_part = values[:, half:]
    return jnp.concatenate(
        [cosine * real_part - sine * imag_part, sine * real_part + cosine * imag_part], axis=1
    )


def pair_face(face, partner):
    phases, comps, tile_a, tile_r = face.shape
    flat = face.reshape(phases, comps, tile_a * tile_r)
    return jnp.take(flat, partner, axis=2).reshape(phases, comps, tile_a, tile_r)


def body(
    psi_start,
    source,
    face_coef,
    diag_coef,
    flux_jac,
    omega,
    metric,
    mode_shape,
    phase_weight,
    pairing,
    owner_order,
):
    matrices = build_matrices(flux_jac)
    comps = matrices.shape[1]
    stacked = matrices.reshape(6 * comps, comps)
    coef = face_coef.astype(jnp.float32)
    local_phases, _, tile_a, tile_r, pitch = psi_start.shape
    first = lax.axis_index("phase") * local_phases
    angle = (first + jnp.arange(local_phases, dtype=jnp.int32)).astype(jnp.float32) * (
        2.0 * math.pi / BLADES
    )
    half = comps // 2
    partner = pairing[0, 0]
    psi = psi_start
    for section in range(ITERS):
        flat = psi.reshape(local_phases, comps, tile_a * tile_r * pitch)
        applied = jnp.einsum("yc,pcn->pyn", stacked, flat, precision=lax.Precision.HIGHEST)
        applied = applied.reshape(local_phases, 6, comps, tile_a, tile_r, pitch)
        parts = [applied[:, d] * coef[d][None, None] for d in range(6)]
        axial_edge = jnp.concatenate([parts[1][:, :, :1], parts[0][:, :, -1:]], axis=2)
        radial_edge = jnp.concatenate([parts[3][:, :, :, :1], parts[2][:, :, :, -1:]], axis=3)
        axial_got = padded(axial_edge, (("axial", 2),), 1)
        radial_got = padded(radial_edge, (("radial", 3),), 1)
        plus_wrap = rotate(pair_face(parts[4][..., -1], partner), angle)
        minus_wrap = rotate(pair_face(parts[5][..., 0], partner), -angle)
        from_lower_a = jnp.concatenate([axial_got[:, :, 0:1], parts[0][:, :, :-1]], axis=2)
        from_upper_a = jnp.concatenate([parts[1][:, :, 1:], axial_got[:, :, 3:4]], axis=2)
        from_lower_r = jnp.concatenate([radial_got[:, :, :, 0:1], parts[2][:, :, :, :-1]], axis=3)
        from_upper_r = jnp.concatenate([parts[3][:, :, :, 1:], radial_got[:, :, :, 3:4]], axis=3)
        from_lower_t = jnp.concatenate([plus_wrap[..., None], parts[4][..., :-1]], axis=4)
        from_upper_t = jnp.concatenate([parts[5][..., 1:], minus_wrap[..., None]], axis=4)
        swapped = jnp.concatenate([psi[:, half:], -psi[:, :half]], axis=1)
        residual = (
            source
            - (diag_coef * psi + omega[0] * swapped)
            + (
                from_lower_a
                + from_upper_a
                + from_lower_r
                + from_upper_r
                + from_lower_t
                + from_upper_t
            )
        )
        psi = psi + RELAX * residual / diag_coef
    cells = tile_a * tile_r * pitch
    heights = jnp.einsum(
        "dc,pcn->pdn",
        metric,
        psi.reshape(local_phases, comps, cells),
        precision=lax.Precision.HIGHEST,
    )
    weighted = jnp.sum(phase_weight[:, None, None] * heights, axis=0)
    order = owner_order[0, 0]
    owned = cells // lax.axis_size("phase")
    count_k = mode_shape.shape[0]
    modes = mode_shape.reshape(count_k, 3, cells).astype(jnp.float32)
    total = modes[:, 0] * weighted[0] + modes[:, 1] * weighted[1] + modes[:, 2] * weighted[2]
    ordered = jnp.take(total, order, axis=1)
    sens = lax.psum_scatter(ordered, "phase", scatter_dimension=1, tiled=True)
    return (psi, sens.reshape(count_k, 1, 1, owned))


def solution(mesh):
    return jax.shard_map(
        body,
        mesh=mesh,
        in_specs=(
            P("phase", None, "axial", "radial", None),
            P("phase", None, "axial", "radial", None),
            P(None, "axial", "radial", None),
            P("axial", "radial", None),
            P(),
            P(),
            P(),
            P(None, None, "axial", "radial", None),
            P("phase"),
            P("axial", "radial", None),
            P("axial", "radial", None),
        ),
        out_specs=(P("phase", None, "axial", "radial", None), P(None, "axial", "radial", "phase")),
        check_vma=False,
    )
```

profile of v0, /device:TPU:0, one launch (start us, length us, event | category | flops | bytes accessed | tf_op | source)
XLA Modules:
  0.0 238.2 jit_solution(10872287852660140842)
XLA Ops:
  9.5 1.8 fusion.84
  13.3 5.5 %collective-permute-start = (f32[1,10,1,16,128]{4,3,2,1,0:T(8,128)}, f32[1,10,1,16,128]{4,3,2,1,0:T(8,128)}, u32[]{:S(2)}, u32[]{:S(2)}) collective-permute-start(f32[1,10,1,16,128]{4,3,2,1,0:T(8,128)} %slice.481), channel_id=1, source_target_pairs={{0,4},{1,5},{2,6},{3,7},{8,12},{9,13},{10,14},{11,15},{16,20},{17,... | collective-permute-start | bytes 245768 | tf_op jit(solution)/shard_map/ppermute | solution.py:22
  21.3 4.1 %collective-permute-start.2 = (f32[1,10,4,1,128]{4,3,2,1,0:T(1,128)}, f32[1,10,4,1,128]{4,3,2,1,0:T(1,128)}, u32[]{:S(2)}, u32[]{:S(2)}) collective-permute-start(f32[1,10,4,1,128]{4,3,2,1,0:T(1,128)} %slice.489), channel_id=1, source_target_pairs={{0,1},{1,2},{2,3},{4,5},{5,6},{6,7},{8,9},{9,10},{10,11},{12,13},{... | collective-permute-start | bytes 61448 | tf_op jit(solution)/shard_map/ppermute | solution.py:22
  42.2 7.4 %copy.274 = f32[12,3,4,16,128]{0,4,3,2,1:T(8,128)} copy(bf16[12,3,4,16,128]{4,3,2,1,0:T(8,128)(2,1)} %param.20) | data formatting | bytes 1769472 | tf_op jit(solution)/shard_map/convert_element_type | solution.py:121
  49.6 1.5 fusion.35
  52.0 1.8 fusion.85
  58.4 5.8 %collective-permute-start.4 = (f32[1,10,1,16,128]{4,3,2,1,0:T(8,128)}, f32[1,10,1,16,128]{4,3,2,1,0:T(8,128)}, u32[]{:S(2)}, u32[]{:S(2)}) collective-permute-start(f32[1,10,1,16,128]{4,3,2,1,0:T(8,128)} %slice.510), channel_id=1, source_target_pairs={{0,4},{1,5},{2,6},{3,7},{8,12},{9,13},{10,14},{11,15},{16,20},{17,... | collective-permute-start | bytes 245768 | tf_op jit(solution)/shard_map/ppermute | solution.py:22
  66.8 5.1 %collective-permute-start.6 = (f32[1,10,4,1,128]{4,3,2,1,0:T(1,128)}, f32[1,10,4,1,128]{4,3,2,1,0:T(1,128)}, u32[]{:S(2)}, u32[]{:S(2)}) collective-permute-start(f32[1,10,4,1,128]{4,3,2,1,0:T(1,128)} %slice.516), channel_id=1, source_target_pairs={{0,1},{1,2},{2,3},{4,5},{5,6},{6,7},{8,9},{9,10},{10,11},{12,13},{... | collective-permute-start | bytes 61448 | tf_op jit(solution)/shard_map/ppermute | solution.py:22
  72.5 1.5 collective-permute-start.7
  78.5 1.5 fusion.45
  80.9 1.8 fusion.86
  87.3 5.8 %collective-permute-start.8 = (f32[1,10,1,16,128]{4,3,2,1,0:T(8,128)}, f32[1,10,1,16,128]{4,3,2,1,0:T(8,128)}, u32[]{:S(2)}, u32[]{:S(2)}) collective-permute-start(f32[1,10,1,16,128]{4,3,2,1,0:T(8,128)} %slice.534), channel_id=1, source_target_pairs={{0,4},{1,5},{2,6},{3,7},{8,12},{9,13},{10,14},{11,15},{16,20},{17,... | collective-permute-start | bytes 245768 | tf_op jit(solution)/shard_map/ppermute | solution.py:22
  95.7 4.2 %collective-permute-start.10 = (f32[1,10,4,1,128]{4,3,2,1,0:T(1,128)}, f32[1,10,4,1,128]{4,3,2,1,0:T(1,128)}, u32[]{:S(2)}, u32[]{:S(2)}) collective-permute-start(f32[1,10,4,1,128]{4,3,2,1,0:T(1,128)} %slice.540), channel_id=1, source_target_pairs={{0,1},{1,2},{2,3},{4,5},{5,6},{6,7},{8,9},{9,10},{10,11},{12,13},{... | collective-permute-start | bytes 61448 | tf_op jit(solution)/shard_map/ppermute | solution.py:22
  106.4 1.5 fusion.55
  108.8 1.8 fusion.87
  115.2 5.8 %collective-permute-start.12 = (f32[1,10,1,16,128]{4,3,2,1,0:T(8,128)}, f32[1,10,1,16,128]{4,3,2,1,0:T(8,128)}, u32[]{:S(2)}, u32[]{:S(2)}) collective-permute-start(f32[1,10,1,16,128]{4,3,2,1,0:T(8,128)} %slice.558), channel_id=1, source_target_pairs={{0,4},{1,5},{2,6},{3,7},{8,12},{9,13},{10,14},{11,15},{16,20},{17,... | collective-permute-start | bytes 245768 | tf_op jit(solution)/shard_map/ppermute | solution.py:22
  123.0 4.0 %collective-permute-start.14 = (f32[1,10,4,1,128]{4,3,2,1,0:T(1,128)S(1)}, f32[1,10,4,1,128]{4,3,2,1,0:T(1,128)}, u32[]{:S(2)}, u32[]{:S(2)}) collective-permute-start(f32[1,10,4,1,128]{4,3,2,1,0:T(1,128)S(1)} %slice.564), channel_id=1, source_target_pairs={{0,1},{1,2},{2,3},{4,5},{5,6},{6,7},{8,9},{9,10},{10,11},{12,13},{... | collective-permute-start | bytes 61448 | tf_op jit(solution)/shard_map/ppermute | solution.py:22
  129.8 3.8 %collective-permute-done.15 = f32[1,10,4,1,128]{4,3,2,1,0:T(1,128)} collective-permute-done((f32[1,10,4,1,128]{4,3,2,1,0:T(1,128)}, f32[1,10,4,1,128]{4,3,2,1,0:T(1,128)}, u32[]{:S(2)}, u32[]{:S(2)}) %collective-permute-start.15) | collective-permute-done | bytes 20512 | tf_op jit(solution)/shard_map/ppermute | solution.py:23
  133.6 1.5 fusion.65
  135.8 9.9 %fusion.2 = f32[12,8192]{0,1:T(8,128)} fusion(f32[12,3,8192]{0,2,1:T(8,128)} %bitcast.340, f32[8192]{0:T(1024)S(1)} %bitcast.385, f32[8192]{0:T(1024)S(1)} %bitcast.386, f32[8192]{0:T(1024)S(1)} %bitcast.384), kind=kLoop, calls=%fused_computation.13 | loop fusion | flops 491520 | bytes 1671168 | tf_op jit(solution)/shard_map/add | solution.py:122
  145.6 30.1 %gather_fusion = f32[8192,12]{1,0:T(8,128)} fusion(f32[12,8192]{0,1:T(8,128)} %fusion.2, s32[8192]{0:T(1024)S(1)} %copy-done.20), kind=kCustom, calls=%fused_computation.8 | custom fusion | bytes 819200 | tf_op jit(solution)/shard_map/jit(_take)/gather | solution.py:123
  175.7 7.4 %select_bitcast_fusion = f32[12,8192]{0,1:T(8,128)} fusion(f32[8192,12]{1,0:T(8,128)} %gather_fusion, pred[8192]{0:T(1024)(128)(4,1)S(1)} %copy-done.22), kind=kLoop, calls=%fused_computation.19 | loop fusion | flops 98304 | bytes 794624 | tf_op jit(solution)/shard_map/jit(_take)/select_n | solution.py:123
  183.2 45.9 %reduce-scatter.2.cloned.1.call-done = f32[12,2048]{0,1:T(8,128)} async-done(((f32[12,8192]{0,1:T(8,128)}), f32[12,2048]{0,1:T(8,128)}) %reduce-scatter.2.cloned.1.call-update) | async-done | bytes 98320 | tf_op jit(solution)/shard_map/reduce_scatter | solution.py:124
  229.1 2.2 copy.275
  (220 shorter events, 59.8 us)
Async XLA Ops:
  7.2 128.1 %copy-start = (f32[3,10]{1,0:T(4,128)S(1)}, f32[3,10]{1,0:T(4,128)}, u32[]{:S(2)}) copy-start(f32[3,10]{1,0:T(4,128)} %param.19) | copy-start | bytes 364
  7.2 221.9 %reduce-scatter.2.cloned.1.call-start = ((), (), s32[]{:S(2)}) async-start(), calls=%async_computation.1 | async-start | bytes 5242880 | tf_op jit(solution)/shard_map/reduce_scatter | solution.py:124
  12.3 25.9 %copy-start.7 = (f32[4,16,128]{2,1,0:T(8,128)}, f32[4,16,128]{2,1,0:T(8,128)S(1)}, u32[]{:S(2)}) copy-start(f32[4,16,128]{2,1,0:T(8,128)S(1)} %get-tuple-element.48) | copy-start | bytes 98308
  12.3 25.9 %copy-start.11 = (f32[4,16,128]{2,1,0:T(8,128)}, f32[4,16,128]{2,1,0:T(8,128)S(1)}, u32[]{:S(2)}) copy-start(f32[4,16,128]{2,1,0:T(8,128)S(1)} %get-tuple-element.49) | copy-start | bytes 98308
  12.3 25.9 %copy-start.15 = (f32[4,16,128]{2,1,0:T(8,128)}, f32[4,16,128]{2,1,0:T(8,128)S(1)}, u32[]{:S(2)}) copy-start(f32[4,16,128]{2,1,0:T(8,128)S(1)} %get-tuple-element.44) | copy-start | bytes 98308
  12.5 18.7 %copy-start.3 = (f32[1,10,4,16,128]{4,3,2,1,0:T(8,128)}, f32[1,10,4,16,128]{4,3,2,1,0:T(8,128)S(1)}, u32[]{:S(2)}) copy-start(f32[1,10,4,16,128]{4,3,2,1,0:T(8,128)S(1)} %get-tuple-element.32) | copy-start | bytes 983044
  13.3 36.4 %collective-permute-start = (f32[1,10,1,16,128]{4,3,2,1,0:T(8,128)}, f32[1,10,1,16,128]{4,3,2,1,0:T(8,128)}, u32[]{:S(2)}, u32[]{:S(2)}) collective-permute-start(f32[1,10,1,16,128]{4,3,2,1,0:T(8,128)} %slice.481), channel_id=1, source_target_pairs={{0,4},{1,5},{2,6},{3,7},{8,12},{9,13},{10,14},{11,15},{16,20},{17,... | collective-permute-start | bytes 245768 | tf_op jit(solution)/shard_map/ppermute | solution.py:22
  19.4 30.3 %collective-permute-start.1 = (f32[1,10,1,16,128]{4,3,2,1,0:T(8,128)}, f32[1,10,1,16,128]{4,3,2,1,0:T(8,128)}, u32[]{:S(2)}, u32[]{:S(2)}) collective-permute-start(f32[1,10,1,16,128]{4,3,2,1,0:T(8,128)} %slice.486), channel_id=1, source_target_pairs={{4,0},{5,1},{6,2},{7,3},{12,8},{13,9},{14,10},{15,11},{20,16},{21,... | collective-permute-start | bytes 245768 | tf_op jit(solution)/shard_map/ppermute | solution.py:23
  21.3 28.3 %collective-permute-start.2 = (f32[1,10,4,1,128]{4,3,2,1,0:T(1,128)}, f32[1,10,4,1,128]{4,3,2,1,0:T(1,128)}, u32[]{:S(2)}, u32[]{:S(2)}) collective-permute-start(f32[1,10,4,1,128]{4,3,2,1,0:T(1,128)} %slice.489), channel_id=1, source_target_pairs={{0,1},{1,2},{2,3},{4,5},{5,6},{6,7},{8,9},{9,10},{10,11},{12,13},{... | collective-permute-start | bytes 61448 | tf_op jit(solution)/shard_map/ppermute | solution.py:22
  26.0 23.7 %collective-permute-start.3 = (f32[1,10,4,1,128]{4,3,2,1,0:T(1,128)}, f32[1,10,4,1,128]{4,3,2,1,0:T(1,128)}, u32[]{:S(2)}, u32[]{:S(2)}) collective-permute-start(f32[1,10,4,1,128]{4,3,2,1,0:T(1,128)} %slice.494), channel_id=1, source_target_pairs={{1,0},{2,1},{3,2},{5,4},{6,5},{7,6},{9,8},{10,9},{11,10},{13,12},{... | collective-permute-start | bytes 61448 | tf_op jit(solution)/shard_map/ppermute | solution.py:23
  58.4 20.1 %collective-permute-start.4 = (f32[1,10,1,16,128]{4,3,2,1,0:T(8,128)}, f32[1,10,1,16,128]{4,3,2,1,0:T(8,128)}, u32[]{:S(2)}, u32[]{:S(2)}) collective-permute-start(f32[1,10,1,16,128]{4,3,2,1,0:T(8,128)} %slice.510), channel_id=1, source_target_pairs={{0,4},{1,5},{2,6},{3,7},{8,12},{9,13},{10,14},{11,15},{16,20},{17,... | collective-permute-start | bytes 245768 | tf_op jit(solution)/shard_map/ppermute | solution.py:22
  64.9 13.6 %collective-permute-start.5 = (f32[1,10,1,16,128]{4,3,2,1,0:T(8,128)}, f32[1,10,1,16,128]{4,3,2,1,0:T(8,128)}, u32[]{:S(2)}, u32[]{:S(2)}) collective-permute-start(f32[1,10,1,16,128]{4,3,2,1,0:T(8,128)} %slice.514), channel_id=1, source_target_pairs={{4,0},{5,1},{6,2},{7,3},{12,8},{13,9},{14,10},{15,11},{20,16},{21,... | collective-permute-start | bytes 245768 | tf_op jit(solution)/shard_map/ppermute | solution.py:23
  66.8 10.8 %collective-permute-start.6 = (f32[1,10,4,1,128]{4,3,2,1,0:T(1,128)}, f32[1,10,4,1,128]{4,3,2,1,0:T(1,128)}, u32[]{:S(2)}, u32[]{:S(2)}) collective-permute-start(f32[1,10,4,1,128]{4,3,2,1,0:T(1,128)} %slice.516), channel_id=1, source_target_pairs={{0,1},{1,2},{2,3},{4,5},{5,6},{6,7},{8,9},{9,10},{10,11},{12,13},{... | collective-permute-start | bytes 61448 | tf_op jit(solution)/shard_map/ppermute | solution.py:22
  72.5 6.0 %collective-permute-start.7 = (f32[1,10,4,1,128]{4,3,2,1,0:T(1,128)}, f32[1,10,4,1,128]{4,3,2,1,0:T(1,128)}, u32[]{:S(2)}, u32[]{:S(2)}) collective-permute-start(f32[1,10,4,1,128]{4,3,2,1,0:T(1,128)} %slice.520), channel_id=1, source_target_pairs={{1,0},{2,1},{3,2},{5,4},{6,5},{7,6},{9,8},{10,9},{11,10},{13,12},{... | collective-permute-start | bytes 61448 | tf_op jit(solution)/shard_map/ppermute | solution.py:23
  87.3 19.1 %collective-permute-start.8 = (f32[1,10,1,16,128]{4,3,2,1,0:T(8,128)}, f32[1,10,1,16,128]{4,3,2,1,0:T(8,128)}, u32[]{:S(2)}, u32[]{:S(2)}) collective-permute-start(f32[1,10,1,16,128]{4,3,2,1,0:T(8,128)} %slice.534), channel_id=1, source_target_pairs={{0,4},{1,5},{2,6},{3,7},{8,12},{9,13},{10,14},{11,15},{16,20},{17,... | collective-permute-start | bytes 245768 | tf_op jit(solution)/shard_map/ppermute | solution.py:22
  93.7 12.7 %collective-permute-start.9 = (f32[1,10,1,16,128]{4,3,2,1,0:T(8,128)}, f32[1,10,1,16,128]{4,3,2,1,0:T(8,128)}, u32[]{:S(2)}, u32[]{:S(2)}) collective-permute-start(f32[1,10,1,16,128]{4,3,2,1,0:T(8,128)} %slice.538), channel_id=1, source_target_pairs={{4,0},{5,1},{6,2},{7,3},{12,8},{13,9},{14,10},{15,11},{20,16},{21,... | collective-permute-start | bytes 245768 | tf_op jit(solution)/shard_map/ppermute | solution.py:23
  95.7 9.6 %collective-permute-start.10 = (f32[1,10,4,1,128]{4,3,2,1,0:T(1,128)}, f32[1,10,4,1,128]{4,3,2,1,0:T(1,128)}, u32[]{:S(2)}, u32[]{:S(2)}) collective-permute-start(f32[1,10,4,1,128]{4,3,2,1,0:T(1,128)} %slice.540), channel_id=1, source_target_pairs={{0,1},{1,2},{2,3},{4,5},{5,6},{6,7},{8,9},{9,10},{10,11},{12,13},{... | collective-permute-start | bytes 61448 | tf_op jit(solution)/shard_map/ppermute | solution.py:22
  100.4 6.0 %collective-permute-start.11 = (f32[1,10,4,1,128]{4,3,2,1,0:T(1,128)}, f32[1,10,4,1,128]{4,3,2,1,0:T(1,128)}, u32[]{:S(2)}, u32[]{:S(2)}) collective-permute-start(f32[1,10,4,1,128]{4,3,2,1,0:T(1,128)} %slice.544), channel_id=1, source_target_pairs={{1,0},{2,1},{3,2},{5,4},{6,5},{7,6},{9,8},{10,9},{11,10},{13,12},{... | collective-permute-start | bytes 61448 | tf_op jit(solution)/shard_map/ppermute | solution.py:23
  111.6 22.0 %copy-start.19 = (f32[4,16,128]{2,1,0:T(8,128)S(1)}, f32[4,16,128]{2,1,0:T(8,128)}, u32[]{:S(2)}) copy-start(f32[4,16,128]{2,1,0:T(8,128)} %param.16) | copy-start | bytes 98308
  115.2 18.4 %collective-permute-start.12 = (f32[1,10,1,16,128]{4,3,2,1,0:T(8,128)}, f32[1,10,1,16,128]{4,3,2,1,0:T(8,128)}, u32[]{:S(2)}, u32[]{:S(2)}) collective-permute-start(f32[1,10,1,16,128]{4,3,2,1,0:T(8,128)} %slice.558), channel_id=1, source_target_pairs={{0,4},{1,5},{2,6},{3,7},{8,12},{9,13},{10,14},{11,15},{16,20},{17,... | collective-permute-start | bytes 245768 | tf_op jit(solution)/shard_map/ppermute | solution.py:22
  121.7 11.9 %collective-permute-start.13 = (f32[1,10,1,16,128]{4,3,2,1,0:T(8,128)}, f32[1,10,1,16,128]{4,3,2,1,0:T(8,128)}, u32[]{:S(2)}, u32[]{:S(2)}) collective-permute-start(f32[1,10,1,16,128]{4,3,2,1,0:T(8,128)} %slice.562), channel_id=1, source_target_pairs={{4,0},{5,1},{6,2},{7,3},{12,8},{13,9},{14,10},{15,11},{20,16},{21,... | collective-permute-start | bytes 245768 | tf_op jit(solution)/shard_map/ppermute | solution.py:23
  123.0 6.8 %collective-permute-start.14 = (f32[1,10,4,1,128]{4,3,2,1,0:T(1,128)S(1)}, f32[1,10,4,1,128]{4,3,2,1,0:T(1,128)}, u32[]{:S(2)}, u32[]{:S(2)}) collective-permute-start(f32[1,10,4,1,128]{4,3,2,1,0:T(1,128)S(1)} %slice.564), channel_id=1, source_target_pairs={{0,1},{1,2},{2,3},{4,5},{5,6},{6,7},{8,9},{9,10},{10,11},{12,13},{... | collective-permute-start | bytes 61448 | tf_op jit(solution)/shard_map/ppermute | solution.py:22
  127.6 6.0 %collective-permute-start.15 = (f32[1,10,4,1,128]{4,3,2,1,0:T(1,128)}, f32[1,10,4,1,128]{4,3,2,1,0:T(1,128)}, u32[]{:S(2)}, u32[]{:S(2)}) collective-permute-start(f32[1,10,4,1,128]{4,3,2,1,0:T(1,128)} %slice.568), channel_id=1, source_target_pairs={{1,0},{2,1},{3,2},{5,4},{6,5},{7,6},{9,8},{10,9},{11,10},{13,12},{... | collective-permute-start | bytes 61448 | tf_op jit(solution)/shard_map/ppermute | solution.py:23
  145.6 30.1 %copy-start.22 = (pred[8192]{0:T(1024)(128)(4,1)S(1)}, pred[8192]{0:T(1024)(128)(4,1)}, u32[]{:S(2)}) copy-start(pred[8192]{0:T(1024)(128)(4,1)} %compare_and_fusion) | copy-start | bytes 24580
  (20 other events, 89.3 us)
Sparse Core Ops, SparseCore 0:
  183.3 45.7 reduce-scatter.1
where the time goes:
time: 240 us; the launch traced here: 238 us
  local copies, waits for them, and re-layouts  77.1 us (32%)
  waiting for transfers between devices  51.9 us (22%)
  starting transfers between devices  50.7 us (21%)
  other arithmetic  34.2 us (14%)
  between operations  16.5 us (7%)
  matrix products  7.76 us (3%)
    reduce_scatter x1, waiting for transfers between devices, body(): sens = lax.psum_scatter(ordered, 'phase', scatter_dimension=1, tiled=True)  45.9 us
    ppermute x8, starting transfers between devices, padded(): before = lax.ppermute(last, axis, up)  40.3 us
    gather x1, local copies, waits for them, and re-layouts, body(): ordered = jnp.take(total, order, axis=1)  30.1 us
    ppermute x8, starting transfers between devices, padded(): after = lax.ppermute(leading, axis, down)  10.4 us
    add x1, other arithmetic, body(): modes[:, 0] * weighted[0] + modes[:, 1] * weighted[1]  9.87 us
    select_n x2, other arithmetic, body(): ordered = jnp.take(total, order, axis=1)  8.26 us
    convert_element_type x1, local copies, waits for them, and re-layouts, body(): modes = mode_shape.reshape(count_k, 3, cells).astype(jnp.float32)  7.39 us
    dot_general x4, matrix products, body(): jnp.einsum('yc,pcn->pyn', stacked, flat, precision=lax.Precision.HIGHEST)  7.32 us
  transfers between devices with their start and end apart: 17, of which 4 were waited for; matrix products, arithmetic and copies ran while one was open for 15% of the time, Pallas kernels for 0%

commit v1 on v0

v1 whole, which is shorter than its diff:
```python
import functools
import math

import jax
import jax.numpy as jnp
from jax import lax
from jax.experimental import pallas as pl
from jax.experimental.pallas import tpu as pltpu
from jax.sharding import PartitionSpec as P

BLADES = 16
ITERS = 4
RELAX = 0.8
MESH = pl.DeviceIdType.MESH
TILE = 256
TOP = 8


def kernel(
    sizes,
    psi_ref,
    source_ref,
    face_ref,
    diag_ref,
    flux_ref,
    omega_ref,
    metric_ref,
    mode_ref,
    weight_ref,
    pairing_ref,
    owner_ref,
    out_ref,
    sens_ref,
    psi,
    axial_low,
    axial_high,
    radial_sent,
    radial_low,
    radial_high,
    face_sent,
    face_low,
    face_high,
    coef,
    acc,
    inverse,
    wrapped,
    pair_matrix,
    one_hot,
    row_mask,
    modes_owned,
    weighted,
    gathered,
    received,
    matrix,
    send_sem,
    recv_sem,
    face_send_sem,
    face_recv_sem,
    phase_send_sem,
    phase_recv_sem,
):
    n_phase, n_axial, n_radial = sizes
    comps, tile_a, tile_r, pitch = psi_ref.shape
    half = comps // 2
    nodes = tile_a * tile_r
    fold = nodes // 2
    n_tiles = owner_ref.shape[1] // TILE
    own_tiles = n_tiles // n_phase
    n_modes = mode_ref.shape[0]
    phase = lax.axis_index("phase")
    ax = lax.axis_index("axial")
    rad = lax.axis_index("radial")
    has_low = (ax > 0, rad > 0)
    has_high = (ax < n_axial - 1, rad < n_radial - 1)
    rows = pl.ds(TOP, tile_r)

    barrier = pltpu.get_barrier_semaphore()
    for k in range(1, n_phase):
        pl.semaphore_signal(
            barrier,
            inc=1,
            device_id={"phase": lax.rem(phase + k, n_phase)},
            device_id_type=MESH,
        )
    for name, me, low, high in (
        ("axial", ax, has_low[0], has_high[0]),
        ("radial", rad, has_low[1], has_high[1]),
    ):
        @pl.when(low)
        def _():
            pl.semaphore_signal(barrier, inc=1, device_id={name: me - 1}, device_id_type=MESH)

        @pl.when(high)
        def _():
            pl.semaphore_signal(barrier, inc=1, device_id={name: me + 1}, device_id_type=MESH)

    for a in range(tile_a):
        psi[0, a, :, TOP : TOP + tile_r, :] = psi_ref[:, a]
        for d in range(6):
            coef[d, a] = face_ref[d, a].astype(jnp.float32)
    for a in range(tile_a):
        face_sent[2, a : a + 1, :] = coef[2, a, tile_r - 1 : tile_r, :]
        face_sent[3, a : a + 1, :] = coef[3, a, 0:1, :]
    for r in range(tile_r // 4):
        face_sent[0, 4 * r : 4 * r + 4, :] = coef[0, tile_a - 1, 4 * r : 4 * r + 4, :]
        face_sent[1, 4 * r : 4 * r + 4, :] = coef[1, 0, 4 * r : 4 * r + 4, :]

    greeted = n_phase - 1 + sum(jnp.where(flag, 1, 0) for flag in has_low + has_high)
    pl.semaphore_wait(barrier, greeted)

    def axial_copy(s, up):
        return pltpu.make_async_remote_copy(
            src_ref=psi.at[s, tile_a - 1 if up else 0, :, rows, :],
            dst_ref=(axial_low if up else axial_high).at[s],
            send_sem=send_sem.at[s, 0 if up else 1],
            recv_sem=recv_sem.at[s, 0 if up else 1],
            device_id={"axial": ax + 1 if up else ax - 1},
            device_id_type=MESH,
        )

    def radial_copy(s, up):
        return pltpu.make_async_remote_copy(
            src_ref=radial_sent.at[s, 0 if up else 1],
            dst_ref=(radial_low if up else radial_high).at[s],
            send_sem=send_sem.at[s, 2 if up else 3],
            recv_sem=recv_sem.at[s, 2 if up else 3],
            device_id={"radial": rad + 1 if up else rad - 1},
            device_id_type=MESH,
        )

    def face_copy(d):
        name, me = ("axial", ax) if d < 2 else ("radial", rad)
        count = tile_r if d < 2 else tile_a
        up = d % 2 == 0
        return pltpu.make_async_remote_copy(
            src_ref=face_sent.at[d],
            dst_ref=(face_low if up else face_high).at[d // 2],
            send_sem=face_send_sem.at[d],
            recv_sem=face_recv_sem.at[d],
            device_id={name: me + 1 if up else me - 1},
            device_id_type=MESH,
        )

    def start_section(s):
        for up in (True, False):
            @pl.when((has_high if up else has_low)[0])
            def _():
                axial_copy(s, up).start()

        for a in range(tile_a):
            radial_sent[s, 0, :, a, :] = psi[s, a, :, TOP + tile_r - 1, :]
            radial_sent[s, 1, :, a, :] = psi[s, a, :, TOP, :]
        for up in (True, False):
            @pl.when((has_high if up else has_low)[1])
            def _():
                radial_copy(s, up).start()

    start_section(0)
    for d in range(6 - 2):
        @pl.when((has_high if d % 2 == 0 else has_low)[d // 2])
        def _():
            face_copy(d).start()

    for d in range(6):
        for j in range(half):
            for i in range(half):
                at = (d * half + j) * half + i
                real, imag = flux_ref[d, 0, j, i], flux_ref[d, 1, j, i]
                matrix[0, at] = real
                matrix[1, at] = real - imag
                matrix[2, at] = real + imag

    node = lax.broadcasted_iota(jnp.int32, (2 * nodes, nodes), 0)
    partner = jnp.where(node >= nodes, node - nodes, node) == pairing_ref[...]
    pair_matrix[...] = jnp.where(partner, 1.0, 0.0).T.astype(jnp.bfloat16)

    def permuted(value):
        high = value.astype(jnp.bfloat16)
        low = (value - high.astype(jnp.float32)).astype(jnp.bfloat16)
        stacked = jnp.concatenate([high, low], axis=0)
        return jnp.dot(pair_matrix[...], stacked, preferred_element_type=jnp.float32)

    lane = lax.broadcasted_iota(jnp.int32, (tile_r, pitch), 1)
    for d, from_lane in ((4, pitch - 1), (5, 0)):
        partner_face = permuted(coef[d].reshape(nodes, pitch))
        for a in range(tile_a):
            own = jnp.where(
                lane == from_lane, partner_face[a * tile_r : (a + 1) * tile_r], coef[d, a]
            )
            coef[d, a] = pltpu.roll(own, 1 if d == 4 else pitch - 1, 1)

    for a in range(tile_a):
        inverse[a] = RELAX / diag_ref[a]

    angle = 2.0 * math.pi / BLADES
    turn = lax.rem(phase, BLADES)
    cosine = jnp.float32(1.0)
    sine = jnp.float32(0.0)
    for k in range(1, BLADES):
        cosine = jnp.where(turn == k, jnp.float32(math.cos(angle * k)), cosine)
        sine = jnp.where(turn == k, jnp.float32(math.sin(angle * k)), sine)

    def make_one_hot(t, _):
        owner = owner_ref[:, pl.ds(pl.multiple_of(t * TILE, TILE), TILE)]
        row = lax.div(owner, pitch)
        column = owner - row * pitch
        later = row >= fold
        column = jnp.where(later, column + pitch, column)
        row = jnp.where(later, row - fold, row)
        at = lax.broadcasted_iota(jnp.int32, (2 * pitch, TILE), 0)
        one_hot[t] = jnp.where(at == column, 1.0, 0.0).astype(jnp.bfloat16)
        at = lax.broadcasted_iota(jnp.int32, (fold, TILE), 0)
        row_mask[t] = jnp.where(at == row, 1.0, 0.0)
        return 0

    lax.fori_loop(0, n_tiles, make_one_hot, 0)

    def gather_modes(i, _):
        t = phase * own_tiles + i
        for d in range(3):
            for k in range(0, n_modes, 6):
                part = mode_ref[k : k + 6, d].reshape(6, nodes, pitch)
                left = part[:, :fold].reshape(6 * fold, pitch)
                right = part[:, fold:].reshape(6 * fold, pitch)
                picked = jnp.dot(
                    jnp.concatenate([left, right], axis=1),
                    one_hot[t],
                    preferred_element_type=jnp.float32,
                )
                picked = picked.reshape(6, fold, TILE) * row_mask[t][None]
                modes_owned[i, d, k : k + 6, :] = jnp.sum(picked, axis=1)
        return 0

    def apply(d, values, totals):
        first, second, third = totals
        both = [values[j] + values[half + j] for j in range(half)]
        for i in range(half):
            for j in range(half):
                at = (d * half + j) * half + i
                first[i] = first[i] + matrix[0, at] * both[j]
                second[i] = second[i] + matrix[1, at] * values[half + j]
                third[i] = third[i] + matrix[2, at] * values[j]
        return totals

    def read(a):
        return [[acc[k, a, i] for i in range(half)] for k in range(3)]

    def write(a, totals):
        for k in range(3):
            for i in range(half):
                acc[k, a, i] = totals[k][i]

    def section(s, _):
        for c in range(comps):
            whole = psi[s, :, c, TOP : TOP + tile_r, :].reshape(nodes, pitch)
            wrapped[c] = permuted(whole).reshape(tile_a, tile_r, pitch)

        def pitch_part(a, _):
            zero = jnp.zeros((tile_r, pitch), jnp.float32)
            totals = [[zero] * half for _ in range(3)]
            for d, from_lane in ((4, pitch - 1), (5, 0)):
                sign = sine if d == 4 else -sine
                values = [None] * comps
                for j in range(half):
                    real, imag = wrapped[j, a], wrapped[half + j, a]
                    turned = (cosine * real - sign * imag, sign * real + cosine * imag)
                    for c, value in ((j, turned[0]), (half + j, turned[1])):
                        value = jnp.where(
                            lane == from_lane, value, psi[s, a, c, TOP : TOP + tile_r, :]
                        )
                        value = pltpu.roll(value, 1 if d == 4 else pitch - 1, 1)
                        values[c] = coef[d, a] * value
                totals = apply(d, values, totals)
            write(a, totals)
            return 0

        lax.fori_loop(0, tile_a, pitch_part, 0)

        def inner_axial(a, _):
            up = [coef[0, a] * psi[s, a, c, TOP : TOP + tile_r, :] for c in range(comps)]
            write(a + 1, apply(0, up, read(a + 1)))
            down = [
                coef[1, a + 1] * psi[s, a + 1, c, TOP : TOP + tile_r, :] for c in range(comps)
            ]
            write(a, apply(1, down, read(a)))
            return 0

        lax.fori_loop(0, tile_a - 1, inner_axial, 0)
        lax.fori_loop(
            lax.div(own_tiles * s, ITERS), lax.div(own_tiles * (s + 1), ITERS), gather_modes, 0
        )

        for up in (True, False):
            flag = (has_low if up else has_high)[1]
            at = TOP - 1 if up else TOP + tile_r
            got = radial_low if up else radial_high

            @pl.when(flag)
            def _():
                radial_copy(s, up).wait_recv()
                for a in range(tile_a):
                    psi[s, a, :, at, :] = got[s, :, a, :]

            @pl.when(jnp.logical_not(flag))
            def _():
                for a in range(tile_a):
                    psi[s, a, :, at, :] = jnp.zeros((comps, pitch), jnp.float32)

        @pl.when(s == 0)
        def _():
            for d in (2, 3):
                flag = (has_low if d == 2 else has_high)[1]
                got = face_low if d == 2 else face_high

                @pl.when(flag)
                def _():
                    face_copy(d).wait_recv()

                row = lax.broadcasted_iota(jnp.int32, (tile_r, pitch), 0)
                edge = 0 if d == 2 else tile_r - 1
                for a in range(tile_a):
                    moved = pltpu.roll(coef[d, a], 1 if d == 2 else tile_r - 1, 0)
                    coef[d, a] = jnp.where(row == edge, 0.0, moved)

                @pl.when(flag)
                def _():
                    for a in range(tile_a):
                        coef[d, a, edge : edge + 1, :] = got[1, a : a + 1, :]

        def radial_part(a, _):
            totals = read(a)
            for d, at in ((2, TOP - 1), (3, TOP + 1)):
                values = [coef[d, a] * psi[s, a, c, at : at + tile_r, :] for c in range(comps)]
                totals = apply(d, values, totals)
            write(a, totals)
            return 0

        lax.fori_loop(0, tile_a, radial_part, 0)

        for up in (True, False):
            @pl.when((has_low if up else has_high)[0])
            def _():
                @pl.when(s == 0)
                def _():
                    face_copy(0 if up else 1).wait_recv()

                axial_copy(s, up).wait_recv()
                got = axial_low if up else axial_high
                weight = (face_low if up else face_high)[0]
                a = 0 if up else tile_a - 1
                values = [weight * got[s, c] for c in range(comps)]
                write(a, apply(0 if up else 1, values, read(a)))

        omega = omega_ref[0]

        def update(a, _):
            first, second, third = read(a)
            scale = inverse[a]
            for i in range(half):
                real = psi[s, a, i, TOP : TOP + tile_r, :]
                imag = psi[s, a, half + i, TOP : TOP + tile_r, :]
                got_real = source_ref[i, a] - omega * imag + (first[i] - second[i])
                got_imag = source_ref[half + i, a] + omega * real + (first[i] - third[i])
                psi[s + 1, a, i, TOP : TOP + tile_r, :] = (1.0 - RELAX) * real + scale * got_real
                psi[s + 1, a, half + i, TOP : TOP + tile_r, :] = (
                    1.0 - RELAX
                ) * imag + scale * got_imag
            return 0

        lax.fori_loop(0, tile_a, update, 0)

        @pl.when(s + 1 < ITERS)
        def _():
            start_section(s + 1)

        return 0

    lax.fori_loop(0, ITERS, section, 0)

    share = weight_ref[0]
    for a in range(tile_a):
        values = [psi[ITERS, a, c, TOP : TOP + tile_r, :] for c in range(comps)]
        row = (a * tile_r) % fold
        column = pitch * ((a * tile_r) // fold)
        for d in range(3):
            height = metric_ref[d, 0] * values[0]
            for c in range(1, comps):
                height = height + metric_ref[d, c] * values[c]
            height = share * height
            high = height.astype(jnp.bfloat16)
            low = (height - high.astype(jnp.float32)).astype(jnp.bfloat16)
            for part, value in ((0, high), (1, low)):
                at = (part * 3 + d) * fold + row
                weighted[at : at + tile_r, column : column + pitch] = value

    def gather_weighted(t, _):
        picked = jnp.dot(weighted[...], one_hot[t], preferred_element_type=jnp.float32)
        picked = picked.reshape(2, 3, fold, TILE)
        gathered[t] = jnp.sum((picked[0] + picked[1]) * row_mask[t][None], axis=1)
        return 0

    def phase_copy(k):
        peer = lax.rem(phase + k, n_phase)
        return pltpu.make_async_remote_copy(
            src_ref=gathered.at[pl.ds(peer * own_tiles, own_tiles)],
            dst_ref=received.at[k],
            send_sem=phase_send_sem.at[k],
            recv_sem=phase_recv_sem.at[k],
            device_id={"phase": peer},
            device_id_type=MESH,
        )

    for k in list(range(1, n_phase)) + [0]:
        peer = lax.rem(phase + k, n_phase)
        lax.fori_loop(peer * own_tiles, (peer + 1) * own_tiles, gather_weighted, 0)
        if k:
            phase_copy(k).start()

    for a in range(tile_a):
        out_ref[:, a] = psi[ITERS, a, :, TOP : TOP + tile_r, :]

    for k in range(1, n_phase):
        phase_copy(k).wait_recv()

    for i in range(own_tiles):
        total = gathered[phase * own_tiles + i]
        for k in range(1, n_phase):
            total = total + received[k, i]
        result = modes_owned[i, 0] * total[0:1]
        for d in range(1, 3):
            result = result + modes_owned[i, d] * total[d : d + 1]
        sens_ref[:, i * TILE : (i + 1) * TILE] = result

    for k in range(1, n_phase):
        phase_copy(k).wait_send()
    for up in (True, False):
        flags = has_high if up else has_low

        @pl.when(flags[0])
        def _():
            face_copy(0 if up else 1).wait_send()
            for s in range(ITERS):
                axial_copy(s, up).wait_send()

        @pl.when(flags[1])
        def _():
            face_copy(2 if up else 3).wait_send()
            for s in range(ITERS):
                radial_copy(s, up).wait_send()


def body(
    sizes,
    psi_start,
    source,
    face_coef,
    diag_coef,
    flux_jac,
    omega,
    metric,
    mode_shape,
    phase_weight,
    pairing,
    owner_order,
):
    _, comps, tile_a, tile_r, pitch = psi_start.shape
    half = comps // 2
    nodes = tile_a * tile_r
    cells = nodes * pitch
    n_phase = sizes[0]
    n_tiles = cells // TILE
    own_tiles = n_tiles // n_phase
    owned = cells // n_phase
    count_k = mode_shape.shape[0]
    f32, bf16 = jnp.float32, jnp.bfloat16
    vmem = pl.BlockSpec(memory_space=pltpu.VMEM)
    smem = pl.BlockSpec(memory_space=pltpu.SMEM)
    dma = pltpu.SemaphoreType.DMA
    psi_out, sens = pl.pallas_call(
        functools.partial(kernel, sizes),
        out_shape=(
            jax.ShapeDtypeStruct((comps, tile_a, tile_r, pitch), f32),
            jax.ShapeDtypeStruct((count_k, owned), f32),
        ),
        in_specs=[vmem, vmem, vmem, vmem, smem, smem, smem, vmem, smem, vmem, vmem],
        out_specs=(vmem, vmem),
        scratch_shapes=[
            pltpu.VMEM((ITERS + 1, tile_a, comps, tile_r + 2 * TOP, pitch), f32),
            pltpu.VMEM((ITERS, comps, tile_r, pitch), f32),
            pltpu.VMEM((ITERS, comps, tile_r, pitch), f32),
            pltpu.VMEM((ITERS, 2, comps, tile_a, pitch), f32),
            pltpu.VMEM((ITERS, comps, tile_a, pitch), f32),
            pltpu.VMEM((ITERS, comps, tile_a, pitch), f32),
            pltpu.VMEM((4, tile_r, pitch), f32),
            pltpu.VMEM((2, tile_r, pitch), f32),
            pltpu.VMEM((2, tile_r, pitch), f32),
            pltpu.VMEM((6, tile_a, tile_r, pitch), f32),
            pltpu.VMEM((3, tile_a, half, tile_r, pitch), f32),
            pltpu.VMEM((tile_a, tile_r, pitch), f32),
            pltpu.VMEM((comps, tile_a, tile_r, pitch), f32),
            pltpu.VMEM((nodes, 2 * nodes), bf16),
            pltpu.VMEM((n_tiles, 2 * pitch, TILE), bf16),
            pltpu.VMEM((n_tiles, nodes // 2, TILE), f32),
            pltpu.VMEM((own_tiles, 3, count_k, TILE), f32),
            pltpu.VMEM((3 * nodes, 2 * pitch), bf16),
            pltpu.VMEM((n_tiles, 3, TILE), f32),
            pltpu.VMEM((n_phase, own_tiles, 3, TILE), f32),
            pltpu.SMEM((3, 6 * half * half), f32),
            dma((ITERS, 4)),
            dma((ITERS, 4)),
            dma((4,)),
            dma((4,)),
            dma((n_phase,)),
            dma((n_phase,)),
        ],
        compiler_params=pltpu.CompilerParams(
            collective_id=0, has_side_effects=True, vmem_limit_bytes=48 * 1024 * 1024
        ),
    )(
        psi_start[0],
        source[0],
        face_coef,
        diag_coef,
        flux_jac,
        omega,
        metric,
        mode_shape,
        phase_weight,
        pairing[0],
        owner_order[0],
    )
    return (psi_out[None], sens.reshape(count_k, 1, 1, owned))


def solution(mesh):
    sizes = tuple(mesh.shape[name] for name in ("phase", "axial", "radial"))
    return jax.shard_map(
        functools.partial(body, sizes),
        mesh=mesh,
        in_specs=(
            P("phase", None, "axial", "radial", None),
            P("phase", None, "axial", "radial", None),
            P(None, "axial", "radial", None),
            P("axial", "radial", None),
            P(),
            P(),
            P(),
            P(None, None, "axial", "radial", None),
            P("phase"),
            P("axial", "radial", None),
            P("axial", "radial", None),
        ),
        out_specs=(P("phase", None, "axial", "radial", None), P(None, "axial", "radial", "phase")),
        check_vma=False,
    )
```

time: 240 us -> 37.6 us (0.16)
  the two profiles are of different devices: /device:TPU:0 before, /device:TPU:1 now
where the time goes in v1:
time: 37.6 us; the launch traced here: 37.3 us
  Pallas kernels  28.9 us (77%)
  local copies, waits for them, and re-layouts  6.32 us (17%)
  between operations  2 us (5%)
    pallas_call x1, Pallas kernels, body(): pl.pallas_call(functools.partial(kernel, sizes), out_shape=(jax.ShapeDtyp...  28.9 us
    unnamed x19, local copies, waits for them, and re-layouts  6.32 us

profile of v1, /device:TPU:1, one launch (start us, length us, event | category | flops | bytes accessed | tf_op | source)
XLA Modules:
  0.0 37.3 jit_solution(17850866893204084155)
XLA Ops:
  1.9 0.0 copy-start.4
  1.9 0.0 copy-start.5
  1.9 0.0 copy-start.6
  2.0 0.0 copy-start.7
  2.0 0.9 %copy.13.flux_ref = f32[6,2,5,5]{3,2,1,0:T(8,128)S(1)} copy(f32[6,2,5,5]{0,1,3,2:T(2,128)} %param.15) | data formatting | bytes 2400 | tf_op args[4]
  2.9 0.0 copy-done.4
  2.9 0.0 copy-done.5
  2.9 0.0 copy-done.6
  2.9 0.0 copy-done.7
  2.9 0.0 copy-start
  3.0 1.1 %copy-done = bf16[12,3,4,16,128]{4,3,2,1,0:T(8,128)(2,1)S(1)} copy-done((bf16[12,3,4,16,128]{4,3,2,1,0:T(8,128)(2,1)S(1)}, bf16[12,3,4,16,128]{4,3,2,1,0:T(8,128)(2,1)}, u32[]{:S(2)}) %copy-start) | copy-done | bytes 589848
  4.0 0.0 copy-start.1
  4.0 1.0 %copy-done.1 = f32[1,10,4,16,128]{4,3,2,1,0:T(8,128)S(1)} copy-done((f32[1,10,4,16,128]{4,3,2,1,0:T(8,128)S(1)}, f32[1,10,4,16,128]{4,3,2,1,0:T(8,128)}, u32[]{:S(2)}) %copy-start.1) | copy-done | bytes 327704
  5.0 0.0 copy-start.2
  5.0 1.0 %copy-done.2 = f32[1,10,4,16,128]{4,3,2,1,0:T(8,128)S(1)} copy-done((f32[1,10,4,16,128]{4,3,2,1,0:T(8,128)S(1)}, f32[1,10,4,16,128]{4,3,2,1,0:T(8,128)}, u32[]{:S(2)}) %copy-start.2) | copy-done | bytes 327704
  6.0 0.0 copy-start.3
  6.0 0.9 %copy-done.3 = bf16[6,4,16,128]{3,2,1,0:T(8,128)(2,1)S(1)} copy-done((bf16[6,4,16,128]{3,2,1,0:T(8,128)(2,1)S(1)}, bf16[6,4,16,128]{3,2,1,0:T(8,128)(2,1)}, u32[]{:S(2)}) %copy-start.3) | copy-done | bytes 98328
  6.8 28.9 %shard_map.122 = (f32[10,4,16,128]{3,2,1,0:T(8,128)S(1)}, f32[12,2048]{1,0:T(8,128)S(1)}) custom-call(f32[10,4,16,128]{3,2,1,0:T(8,128)S(1)} %bitcast.7, f32[10,4,16,128]{3,2,1,0:T(8,128)S(1)} %bitcast.8, bf16[6,4,16,128]{3,2,1,0:T(8,128)(2,1)S(1)} %copy-done.3, f32[4,16,128]{2,1,0:T(8,128)S(1)} %copy-done.4, f32[6,2,5,5]{3,2,1,0:T(8,128)S(1)} %copy.13.flux_ref, ...), custom_call_target="tpu_custom_call" | custom-call | tf_op jit(solution)/shard_map/pallas_call | solution.py:479
  35.8 0.7 %copy.14 = f32[12,1,1,2048]{3,2,1,0:T(1,128)} copy(f32[12,1,1,2048]{3,0,2,1:T(8,128)S(1)} %bitcast.9) | data formatting | bytes 196608
  36.5 0.7 %copy.18 = f32[1,10,4,16,128]{4,3,2,1,0:T(8,128)} copy(f32[1,10,4,16,128]{4,3,2,1,0:T(8,128)S(1)} %bitcast.6) | data formatting | bytes 655360
Async XLA Ops:
  1.9 1.0 %copy-start.4 = (f32[4,16,128]{2,1,0:T(8,128)S(1)}, f32[4,16,128]{2,1,0:T(8,128)}, u32[]{:S(2)}) copy-start(f32[4,16,128]{2,1,0:T(8,128)} %diag_ref.1) | copy-start | bytes 98308
  1.9 1.0 %copy-start.5 = (s32[1,1,8192]{2,1,0:T(1,128)S(1)}, s32[1,1,8192]{2,1,0:T(1,128)}, u32[]{:S(2)}) copy-start(s32[1,1,8192]{2,1,0:T(1,128)} %param.21) | copy-start | bytes 98308
  1.9 1.0 %copy-start.6 = (f32[3,10]{1,0:T(4,128)S(1)}, f32[3,10]{1,0:T(4,128)}, u32[]{:S(2)}) copy-start(f32[3,10]{1,0:T(4,128)} %metric_ref.1) | copy-start | bytes 364
  2.0 1.0 %copy-start.7 = (s32[1,1,64]{2,1,0:T(1,128)S(1)}, s32[1,1,64]{2,1,0:T(1,128)}, u32[]{:S(2)}) copy-start(s32[1,1,64]{2,1,0:T(1,128)} %param.20) | copy-start | bytes 772
  2.9 1.1 %copy-start = (bf16[12,3,4,16,128]{4,3,2,1,0:T(8,128)(2,1)S(1)}, bf16[12,3,4,16,128]{4,3,2,1,0:T(8,128)(2,1)}, u32[]{:S(2)}) copy-start(bf16[12,3,4,16,128]{4,3,2,1,0:T(8,128)(2,1)} %mode_ref.1) | copy-start | bytes 1769476
  4.0 1.0 %copy-start.1 = (f32[1,10,4,16,128]{4,3,2,1,0:T(8,128)S(1)}, f32[1,10,4,16,128]{4,3,2,1,0:T(8,128)}, u32[]{:S(2)}) copy-start(f32[1,10,4,16,128]{4,3,2,1,0:T(8,128)} %param.11) | copy-start | bytes 983044
  5.0 1.0 %copy-start.2 = (f32[1,10,4,16,128]{4,3,2,1,0:T(8,128)S(1)}, f32[1,10,4,16,128]{4,3,2,1,0:T(8,128)}, u32[]{:S(2)}) copy-start(f32[1,10,4,16,128]{4,3,2,1,0:T(8,128)} %param.12) | copy-start | bytes 983044
  6.0 0.9 %copy-start.3 = (bf16[6,4,16,128]{3,2,1,0:T(8,128)(2,1)S(1)}, bf16[6,4,16,128]{3,2,1,0:T(8,128)(2,1)}, u32[]{:S(2)}) copy-start(bf16[6,4,16,128]{3,2,1,0:T(8,128)(2,1)} %face_ref.1) | copy-start | bytes 294916

commit v2 on v1

v2 whole, which is shorter than its diff:
```python
import functools
import math

import jax
import jax.numpy as jnp
from jax import lax
from jax.experimental import pallas as pl
from jax.experimental.pallas import tpu as pltpu
from jax.sharding import PartitionSpec as P

BLADES = 16
ITERS = 4
RELAX = 0.8
MESH = pl.DeviceIdType.MESH
TILE = 256
TOP = 8


def split(value):
    high = value.astype(jnp.bfloat16)
    return high, (value - high.astype(jnp.float32)).astype(jnp.bfloat16)


def kernel(
    sizes,
    psi_in,
    source_in,
    face_in,
    diag_in,
    flux_in,
    omega_ref,
    metric_ref,
    mode_in,
    weight_ref,
    pairing_in,
    owner_in,
    out_ref,
    sens_ref,
    psi,
    source_ref,
    face_ref,
    diag_ref,
    flux_ref,
    mode_ref,
    pairing_ref,
    owner_ref,
    radial_sent,
    radial_low,
    radial_high,
    face_sent,
    face_low,
    face_high,
    coef,
    inverse,
    wrapped,
    pair_matrix,
    matrix,
    field_high,
    field_low,
    one_hot,
    row_mask,
    modes_owned,
    weighted,
    gathered,
    received,
    load_sem,
    send_sem,
    recv_sem,
    face_send_sem,
    face_recv_sem,
    phase_send_sem,
    phase_recv_sem,
):
    n_phase, n_axial, n_radial = sizes
    comps, tile_a, tile_r, pitch = source_ref.shape
    half = comps // 2
    nodes = tile_a * tile_r
    fold = nodes // 2
    n_tiles = owner_ref.shape[1] // TILE
    own_tiles = n_tiles // n_phase
    n_modes = mode_ref.shape[0]
    depth = 6 * comps * TOP
    phase = lax.axis_index("phase")
    ax = lax.axis_index("axial")
    rad = lax.axis_index("radial")
    has_low = (ax > 0, rad > 0)
    has_high = (ax < n_axial - 1, rad < n_radial - 1)
    rows = pl.ds(TOP, tile_r)

    loads = [
        pltpu.make_async_copy(psi_in.at[:, a], psi.at[0, a + 1, :, rows, :], load_sem.at[a])
        for a in range(tile_a)
    ]
    for pair in (
        (face_in, face_ref),
        (flux_in, flux_ref),
        (pairing_in, pairing_ref),
        (diag_in, diag_ref),
        (owner_in, owner_ref),
        (source_in, source_ref),
        (mode_in, mode_ref),
    ):
        loads.append(pltpu.make_async_copy(pair[0], pair[1], load_sem.at[len(loads)]))
    for copy in loads:
        copy.start()

    barrier = pltpu.get_barrier_semaphore()
    for k in range(1, n_phase):
        pl.semaphore_signal(
            barrier,
            inc=1,
            device_id={"phase": lax.rem(phase + k, n_phase)},
            device_id_type=MESH,
        )
    for name, me, low, high in (
        ("axial", ax, has_low[0], has_high[0]),
        ("radial", rad, has_low[1], has_high[1]),
    ):
        @pl.when(low)
        def _():
            pl.semaphore_signal(barrier, inc=1, device_id={name: me - 1}, device_id_type=MESH)

        @pl.when(high)
        def _():
            pl.semaphore_signal(barrier, inc=1, device_id={name: me + 1}, device_id_type=MESH)

    for flag, at, d in ((has_low[0], 0, 0), (has_high[0], tile_a + 1, 1)):
        @pl.when(jnp.logical_not(flag))
        def _():
            coef[d, at] = jnp.zeros((tile_r, pitch), jnp.float32)
            for s in range(ITERS):
                for c in range(comps):
                    psi[s, at, c, TOP : TOP + tile_r, :] = jnp.zeros(
                        (tile_r, pitch), jnp.float32
                    )

    def axial_copy(s, up):
        return pltpu.make_async_remote_copy(
            src_ref=psi.at[s, tile_a if up else 1, :, rows, :],
            dst_ref=psi.at[s, 0 if up else tile_a + 1, :, rows, :],
            send_sem=send_sem.at[s, 0 if up else 1],
            recv_sem=recv_sem.at[s, 0 if up else 1],
            device_id={"axial": ax + 1 if up else ax - 1},
            device_id_type=MESH,
        )

    def radial_copy(s, up):
        return pltpu.make_async_remote_copy(
            src_ref=radial_sent.at[s, 0 if up else 1],
            dst_ref=(radial_low if up else radial_high).at[s],
            send_sem=send_sem.at[s, 2 if up else 3],
            recv_sem=recv_sem.at[s, 2 if up else 3],
            device_id={"radial": rad + 1 if up else rad - 1},
            device_id_type=MESH,
        )

    def face_copy(d):
        up = d % 2 == 0
        if d < 2:
            src = coef.at[d, tile_a if up else 1]
            dst = coef.at[d, 0 if up else tile_a + 1]
            target = {"axial": ax + 1 if up else ax - 1}
        else:
            src = face_sent.at[d - 2]
            dst = face_low if up else face_high
            target = {"radial": rad + 1 if up else rad - 1}
        return pltpu.make_async_remote_copy(
            src_ref=src,
            dst_ref=dst,
            send_sem=face_send_sem.at[d],
            recv_sem=face_recv_sem.at[d],
            device_id=target,
            device_id_type=MESH,
        )

    def start_axial(s):
        for up in (True, False):
            @pl.when((has_high if up else has_low)[0])
            def _():
                axial_copy(s, up).start()

    def start_radial(s):
        for a in range(tile_a):
            radial_sent[s, 0, :, a, :] = psi[s, a + 1, :, TOP + tile_r - 1, :]
            radial_sent[s, 1, :, a, :] = psi[s, a + 1, :, TOP, :]
        for up in (True, False):
            @pl.when((has_high if up else has_low)[1])
            def _():
                radial_copy(s, up).start()

    for copy in loads[:tile_a]:
        copy.wait()
    greeted = n_phase - 1 + sum(jnp.where(flag, 1, 0) for flag in has_low + has_high)
    pl.semaphore_wait(barrier, greeted)
    start_axial(0)
    start_radial(0)

    loads[tile_a].wait()
    for a in range(tile_a):
        for d in range(6):
            coef[d, a + 1] = face_ref[d, a].astype(jnp.float32)
    for a in range(tile_a):
        face_sent[0, a : a + 1, :] = coef[2, a + 1, tile_r - 1 : tile_r, :]
        face_sent[1, a : a + 1, :] = coef[3, a + 1, 0:1, :]
    for d in range(4):
        @pl.when((has_high if d % 2 == 0 else has_low)[d // 2])
        def _():
            face_copy(d).start()

    loads[tile_a + 1].wait()
    real = [flux_ref[j, :, 0, :] for j in range(half)]
    imag = [flux_ref[j, :, 1, :] for j in range(half)]
    fine = lax.Precision.HIGHEST
    entries = (
        jnp.concatenate(real + imag, axis=1),
        jnp.concatenate([-value for value in imag] + real, axis=1),
    )
    tall, wide = comps * TOP, matrix.shape[1]
    spread = jnp.zeros((tall, 6 * comps), jnp.float32)
    row = lax.div(lax.broadcasted_iota(jnp.int32, (tall, half), 0), TOP)
    column = lax.broadcasted_iota(jnp.int32, (tall, half), 1)
    for k in range(2):
        pick = jnp.where(row == column + k * half, 1.0, 0.0)
        spread = spread + jnp.dot(
            pick, entries[k], precision=fine, preferred_element_type=jnp.float32
        )
    row = lax.broadcasted_iota(jnp.int32, (6 * comps, wide), 0)
    column = lax.div(lax.broadcasted_iota(jnp.int32, (6 * comps, wide), 1), TOP)
    spread = jnp.dot(
        spread,
        jnp.where(row == column, 1.0, 0.0),
        precision=fine,
        preferred_element_type=jnp.float32,
    )
    row = lax.rem(lax.broadcasted_iota(jnp.int32, (tall, wide), 0), TOP)
    column = lax.rem(lax.broadcasted_iota(jnp.int32, (tall, wide), 1), TOP)
    high, low = split(jnp.where(row == column, spread, 0.0))
    matrix[:tall] = high
    matrix[tall:] = low
    for slot in range(tile_a):
        for field in (field_high, field_low):
            field[slot, depth:, :] = jnp.zeros((wide - depth, 2 * pitch), jnp.bfloat16)

    loads[tile_a + 2].wait()
    node = lax.broadcasted_iota(jnp.int32, (2 * nodes, nodes), 0)
    partner = jnp.where(node >= nodes, node - nodes, node) == pairing_ref[...]
    pair_matrix[...] = jnp.where(partner, 1.0, 0.0).T.astype(jnp.bfloat16)

    def permuted(value):
        stacked = jnp.concatenate(split(value), axis=0)
        return jnp.dot(pair_matrix[...], stacked, preferred_element_type=jnp.float32)

    lane = lax.broadcasted_iota(jnp.int32, (tile_r, pitch), 1)
    for d, from_lane in ((4, pitch - 1), (5, 0)):
        partner_face = permuted(coef[d, 1 : tile_a + 1].reshape(nodes, pitch))
        for a in range(tile_a):
            own = jnp.where(
                lane == from_lane, partner_face[a * tile_r : (a + 1) * tile_r], coef[d, a + 1]
            )
            coef[d, a + 1] = pltpu.roll(own, 1 if d == 4 else pitch - 1, 1)

    loads[tile_a + 3].wait()
    for a in range(tile_a):
        inverse[a] = RELAX / diag_ref[a]

    angle = 2.0 * math.pi / BLADES
    turn = lax.rem(phase, BLADES)
    cosine = jnp.float32(1.0)
    sine = jnp.float32(0.0)
    for k in range(1, BLADES):
        cosine = jnp.where(turn == k, jnp.float32(math.cos(angle * k)), cosine)
        sine = jnp.where(turn == k, jnp.float32(math.sin(angle * k)), sine)

    def make_one_hot(u, _):
        t = lax.rem(phase * own_tiles + u, n_tiles)
        owner = owner_ref[:, pl.ds(pl.multiple_of(t * TILE, TILE), TILE)]
        row = lax.div(owner, pitch)
        column = owner - row * pitch
        later = row >= fold
        column = jnp.where(later, column + pitch, column)
        row = jnp.where(later, row - fold, row)
        at = lax.broadcasted_iota(jnp.int32, (2 * pitch, TILE), 0)
        one_hot[t] = jnp.where(at == column, 1.0, 0.0).astype(jnp.bfloat16)
        at = lax.broadcasted_iota(jnp.int32, (fold, TILE), 0)
        row_mask[t] = jnp.where(at == row, 1.0, 0.0)
        return 0

    def gather_modes(i, _):
        t = phase * own_tiles + i
        for d in range(3):
            for k in range(0, n_modes, 6):
                part = mode_ref[k : k + 6, d].reshape(6, nodes, pitch)
                left = part[:, :fold].reshape(6 * fold, pitch)
                right = part[:, fold:].reshape(6 * fold, pitch)
                picked = jnp.dot(
                    jnp.concatenate([left, right], axis=1),
                    one_hot[t],
                    preferred_element_type=jnp.float32,
                )
                picked = picked.reshape(6, fold, TILE) * row_mask[t][None]
                modes_owned[i, d, k : k + 6, :] = jnp.sum(picked, axis=1)
        return 0

    def build(s, a, slot):
        for c in range(comps):
            own = psi[s, a, c, TOP : TOP + tile_r, :]
            scaled = (
                coef[0, a - 1] * psi[s, a - 1, c, TOP : TOP + tile_r, :],
                coef[1, a + 1] * psi[s, a + 1, c, TOP : TOP + tile_r, :],
                coef[2, a] * psi[s, a, c, TOP - 1 : TOP + tile_r - 1, :],
                coef[3, a] * psi[s, a, c, TOP + 1 : TOP + tile_r + 1, :],
                coef[4, a] * pltpu.roll(jnp.where(lane == pitch - 1, wrapped[c, a - 1], own), 1, 1),
                coef[5, a]
                * pltpu.roll(jnp.where(lane == 0, wrapped[c, a - 1], own), pitch - 1, 1),
            )
            for d in range(0, 6, 2):
                at = (c * 6 + d) * TOP
                for k in range(2):
                    block = jnp.concatenate(
                        [value[k * TOP : (k + 1) * TOP] for value in scaled[d : d + 2]], axis=0
                    )
                    high, low = split(block)
                    columns = slice(k * pitch, (k + 1) * pitch)
                    field_high[slot, at : at + 2 * TOP, columns] = high
                    field_low[slot, at : at + 2 * TOP, columns] = low

    def update(s, a, slot):
        both = jnp.dot(matrix[...], field_high[slot], preferred_element_type=jnp.float32)
        rest = jnp.dot(matrix[:tall], field_low[slot], preferred_element_type=jnp.float32)
        total = both[:tall] + (both[tall:] + rest)
        omega = omega_ref[0]
        scale = inverse[a - 1]

        def incoming(c):
            part = total[c * TOP : (c + 1) * TOP]
            return jnp.concatenate([part[:, :pitch], part[:, pitch:]], axis=0)

        for i in range(half):
            real = psi[s, a, i, TOP : TOP + tile_r, :]
            imag = psi[s, a, half + i, TOP : TOP + tile_r, :]
            got_real = source_ref[i, a - 1] - omega * imag + incoming(i)
            got_imag = source_ref[half + i, a - 1] + omega * real + incoming(half + i)
            psi[s + 1, a, i, TOP : TOP + tile_r, :] = (1.0 - RELAX) * real + scale * got_real
            psi[s + 1, a, half + i, TOP : TOP + tile_r, :] = (
                1.0 - RELAX
            ) * imag + scale * got_imag

    def wait_axial(s):
        for up in (True, False):
            @pl.when((has_low if up else has_high)[0])
            def _():
                @pl.when(s == 0)
                def _():
                    face_copy(0 if up else 1).wait_recv()

                axial_copy(s, up).wait_recv()

    first = jnp.where(ax > 0, 2, 1)
    turned_sine = jnp.where(lane >= pitch // 2, sine, -sine)

    def section(s, _):
        for c in range(comps):
            whole = psi[s, 1 : tile_a + 1, c, TOP : TOP + tile_r, :].reshape(nodes, pitch)
            wrapped[c] = permuted(whole).reshape(tile_a, tile_r, pitch)
        for a in range(tile_a):
            for j in range(half):
                real, imag = wrapped[j, a], wrapped[half + j, a]
                wrapped[j, a] = cosine * real - turned_sine * imag
                wrapped[half + j, a] = turned_sine * real + cosine * imag

        @pl.when(s == 0)
        def _():
            for copy in loads[tile_a + 4 :]:
                copy.wait()

        lax.fori_loop(
            lax.div(n_tiles * s, ITERS), lax.div(n_tiles * (s + 1), ITERS), make_one_hot, 0
        )
        lax.fori_loop(
            lax.div(own_tiles * s, ITERS), lax.div(own_tiles * (s + 1), ITERS), gather_modes, 0
        )

        for up in (True, False):
            flag = (has_low if up else has_high)[1]
            at = TOP - 1 if up else TOP + tile_r
            got = radial_low if up else radial_high

            @pl.when(flag)
            def _():
                radial_copy(s, up).wait_recv()
                for a in range(tile_a):
                    psi[s, a + 1, :, at, :] = got[s, :, a, :]

            @pl.when(jnp.logical_not(flag))
            def _():
                for a in range(tile_a):
                    psi[s, a + 1, :, at, :] = jnp.zeros((comps, pitch), jnp.float32)

        @pl.when(s == 0)
        def _():
            for d in (2, 3):
                flag = (has_low if d == 2 else has_high)[1]
                got = face_low if d == 2 else face_high

                @pl.when(flag)
                def _():
                    face_copy(d).wait_recv()

                row = lax.broadcasted_iota(jnp.int32, (tile_r, pitch), 0)
                edge = 0 if d == 2 else tile_r - 1
                for a in range(tile_a):
                    moved = pltpu.roll(coef[d, a + 1], 1 if d == 2 else tile_r - 1, 0)
                    coef[d, a + 1] = jnp.where(row == edge, 0.0, moved)

                @pl.when(flag)
                def _():
                    for a in range(tile_a):
                        coef[d, a + 1, edge : edge + 1, :] = got[a : a + 1, :]

        if n_axial > 2:
            wait_axial(s)
        for k in range(tile_a - 1):
            build(s, first + k, k)
        for k in range(tile_a - 1):
            update(s, first + k, k)
        if n_axial <= 2:
            wait_axial(s)
        last = jnp.where(ax > 0, 1, tile_a)
        build(s, last, tile_a - 1)
        update(s, last, tile_a - 1)

        @pl.when(s + 1 < ITERS)
        def _():
            start_axial(s + 1)
            start_radial(s + 1)

        return 0

    lax.fori_loop(0, ITERS, section, 0)

    share = weight_ref[0]
    for a in range(tile_a):
        values = [psi[ITERS, a + 1, c, TOP : TOP + tile_r, :] for c in range(comps)]
        row = (a * tile_r) % fold
        column = pitch * ((a * tile_r) // fold)
        for d in range(3):
            height = metric_ref[d, 0] * values[0]
            for c in range(1, comps):
                height = height + metric_ref[d, c] * values[c]
            for part, value in enumerate(split(share * height)):
                at = (part * 3 + d) * fold + row
                weighted[at : at + tile_r, column : column + pitch] = value

    def gather_weighted(t):
        picked = jnp.dot(weighted[...], one_hot[t], preferred_element_type=jnp.float32)
        picked = picked.reshape(2, 3, fold, TILE)
        gathered[t] = jnp.sum((picked[0] + picked[1]) * row_mask[t][None], axis=1)

    def phase_copy(k):
        peer = lax.rem(phase + k, n_phase)
        return pltpu.make_async_remote_copy(
            src_ref=gathered.at[pl.ds(peer * own_tiles, own_tiles)],
            dst_ref=received.at[k],
            send_sem=phase_send_sem.at[k],
            recv_sem=phase_recv_sem.at[k],
            device_id={"phase": peer},
            device_id_type=MESH,
        )

    for k in list(range(1, n_phase)) + [0]:
        peer = lax.rem(phase + k, n_phase)
        for i in range(own_tiles):
            gather_weighted(peer * own_tiles + i)
        if k:
            phase_copy(k).start()

    for a in range(tile_a):
        out_ref[:, a] = psi[ITERS, a + 1, :, TOP : TOP + tile_r, :]

    for k in range(1, n_phase):
        phase_copy(k).wait_recv()

    for i in range(own_tiles):
        total = gathered[phase * own_tiles + i]
        for k in range(1, n_phase):
            total = total + received[k, i]
        result = modes_owned[i, 0] * total[0:1]
        for d in range(1, 3):
            result = result + modes_owned[i, d] * total[d : d + 1]
        sens_ref[:, i * TILE : (i + 1) * TILE] = result

    for k in range(1, n_phase):
        phase_copy(k).wait_send()
    for up in (True, False):
        flags = has_high if up else has_low

        @pl.when(flags[0])
        def _():
            face_copy(0 if up else 1).wait_send()
            for s in range(ITERS):
                axial_copy(s, up).wait_send()

        @pl.when(flags[1])
        def _():
            face_copy(2 if up else 3).wait_send()
            for s in range(ITERS):
                radial_copy(s, up).wait_send()


def body(
    sizes,
    psi_start,
    source,
    face_coef,
    diag_coef,
    flux_jac,
    omega,
    metric,
    mode_shape,
    phase_weight,
    pairing,
    owner_order,
):
    _, comps, tile_a, tile_r, pitch = psi_start.shape
    half = comps // 2
    nodes = tile_a * tile_r
    cells = nodes * pitch
    n_phase = sizes[0]
    n_tiles = cells // TILE
    own_tiles = n_tiles // n_phase
    owned = cells // n_phase
    count_k = mode_shape.shape[0]
    f32, bf16 = jnp.float32, jnp.bfloat16
    vmem = pl.BlockSpec(memory_space=pltpu.VMEM)
    smem = pl.BlockSpec(memory_space=pltpu.SMEM)
    hbm = pl.BlockSpec(memory_space=pltpu.HBM)
    dma = pltpu.SemaphoreType.DMA
    depth = -(-6 * comps * TOP // 128) * 128
    psi_out, sens = pl.pallas_call(
        functools.partial(kernel, sizes),
        out_shape=(
            jax.ShapeDtypeStruct((comps, tile_a, tile_r, pitch), f32),
            jax.ShapeDtypeStruct((count_k, owned), f32),
        ),
        in_specs=[hbm, hbm, hbm, hbm, hbm, smem, smem, hbm, smem, hbm, hbm],
        out_specs=(vmem, vmem),
        scratch_shapes=[
            pltpu.VMEM((ITERS + 1, tile_a + 2, comps, tile_r + 2 * TOP, pitch), f32),
            pltpu.VMEM((comps, tile_a, tile_r, pitch), f32),
            pltpu.VMEM((6, tile_a, tile_r, pitch), bf16),
            pltpu.VMEM((tile_a, tile_r, pitch), f32),
            pltpu.VMEM((half, half, 2, 6), f32),
            pltpu.VMEM((count_k, 3, tile_a, tile_r, pitch), bf16),
            pltpu.VMEM((1, nodes), jnp.int32),
            pltpu.VMEM((1, cells), jnp.int32),
            pltpu.VMEM((ITERS, 2, comps, tile_a, pitch), f32),
            pltpu.VMEM((ITERS, comps, tile_a, pitch), f32),
            pltpu.VMEM((ITERS, comps, tile_a, pitch), f32),
            pltpu.VMEM((2, tile_a, pitch), f32),
            pltpu.VMEM((tile_a, pitch), f32),
            pltpu.VMEM((tile_a, pitch), f32),
            pltpu.VMEM((6, tile_a + 2, tile_r, pitch), f32),
            pltpu.VMEM((tile_a, tile_r, pitch), f32),
            pltpu.VMEM((comps, tile_a, tile_r, pitch), f32),
            pltpu.VMEM((nodes, 2 * nodes), bf16),
            pltpu.VMEM((2 * comps * TOP, depth), bf16),
            pltpu.VMEM((tile_a, depth, 2 * pitch), bf16),
            pltpu.VMEM((tile_a, depth, 2 * pitch), bf16),
            pltpu.VMEM((n_tiles, 2 * pitch, TILE), bf16),
            pltpu.VMEM((n_tiles, nodes // 2, TILE), f32),
            pltpu.VMEM((own_tiles, 3, count_k, TILE), f32),
            pltpu.VMEM((3 * nodes, 2 * pitch), bf16),
            pltpu.VMEM((n_tiles, 3, TILE), f32),
            pltpu.VMEM((n_phase, own_tiles, 3, TILE), f32),
            dma((tile_a + 7,)),
            dma((ITERS, 4)),
            dma((ITERS, 4)),
            dma((4,)),
            dma((4,)),
            dma((n_phase,)),
            dma((n_phase,)),
        ],
        compiler_params=pltpu.CompilerParams(
            collective_id=0, has_side_effects=True, vmem_limit_bytes=48 * 1024 * 1024
        ),
    )(
        psi_start[0],
        source[0],
        face_coef,
        diag_coef,
        jnp.transpose(flux_jac, (2, 3, 1, 0)),
        omega,
        metric,
        mode_shape,
        phase_weight,
        pairing[0],
        owner_order[0],
    )
    return (psi_out[None], sens.reshape(count_k, 1, 1, owned))


def solution(mesh):
    sizes = tuple(mesh.shape[name] for name in ("phase", "axial", "radial"))
    return jax.shard_map(
        functools.partial(body, sizes),
        mesh=mesh,
        in_specs=(
            P("phase", None, "axial", "radial", None),
            P("phase", None, "axial", "radial", None),
            P(None, "axial", "radial", None),
            P("axial", "radial", None),
            P(),
            P(),
            P(),
            P(None, None, "axial", "radial", None),
            P("phase"),
            P("axial", "radial", None),
            P("axial", "radial", None),
        ),
        out_specs=(P("phase", None, "axial", "radial", None), P(None, "axial", "radial", "phase")),
        check_vma=False,
    )
```

time: 37.6 us -> 36.7 us (0.976)
  the two profiles are of different devices: /device:TPU:1 before, /device:TPU:0 now
where the time goes in v2:
time: 36.7 us; the launch traced here: 36.2 us
  Pallas kernels  26 us (71%)
  local copies, waits for them, and re-layouts  8.29 us (23%)
  between operations  1.96 us (5%)
    pallas_call x1, Pallas kernels, body(): pl.pallas_call(functools.partial(kernel, sizes), out_shape=(jax.ShapeDtyp...  26 us
    unnamed x20, local copies, waits for them, and re-layouts  8.29 us

profile of v2, /device:TPU:0, one launch (start us, length us, event | category | flops | bytes accessed | tf_op | source)
XLA Modules:
  0.0 36.2 jit_solution(16684855401730477636)
XLA Ops:
  1.9 0.0 copy-start.7
  1.9 0.0 copy-start.8
  1.9 0.7 %copy-done.7 = f32[3,10]{1,0:T(4,128)S(1)} copy-done((f32[3,10]{1,0:T(4,128)S(1)}, f32[3,10]{1,0:T(4,128)}, u32[]{:S(2)}) %copy-start.7) | copy-done | bytes 144
  2.6 0.0 copy-done.8
  2.6 0.0 copy-start
  2.6 1.1 %copy-done = bf16[12,3,4,16,128]{4,3,2,1,0:T(8,128)(2,1)S(1)} copy-done((bf16[12,3,4,16,128]{4,3,2,1,0:T(8,128)(2,1)S(1)}, bf16[12,3,4,16,128]{4,3,2,1,0:T(8,128)(2,1)}, u32[]{:S(2)}) %copy-start) | copy-done | bytes 589848
  3.7 0.0 copy-start.1
  3.7 1.0 %copy-done.1 = f32[1,10,4,16,128]{4,3,2,1,0:T(8,128)S(1)} copy-done((f32[1,10,4,16,128]{4,3,2,1,0:T(8,128)S(1)}, f32[1,10,4,16,128]{4,3,2,1,0:T(8,128)}, u32[]{:S(2)}) %copy-start.1) | copy-done | bytes 327704
  4.6 0.0 copy-start.2
  4.7 1.0 %copy-done.2 = f32[1,10,4,16,128]{4,3,2,1,0:T(8,128)S(1)} copy-done((f32[1,10,4,16,128]{4,3,2,1,0:T(8,128)S(1)}, f32[1,10,4,16,128]{4,3,2,1,0:T(8,128)}, u32[]{:S(2)}) %copy-start.2) | copy-done | bytes 327704
  5.6 0.0 copy-start.3
  5.6 0.9 %copy-done.3 = bf16[6,4,16,128]{3,2,1,0:T(8,128)(2,1)S(1)} copy-done((bf16[6,4,16,128]{3,2,1,0:T(8,128)(2,1)S(1)}, bf16[6,4,16,128]{3,2,1,0:T(8,128)(2,1)}, u32[]{:S(2)}) %copy-start.3) | copy-done | bytes 98328
  6.5 0.0 copy-start.4
  6.5 0.8 %copy-done.4 = f32[4,16,128]{2,1,0:T(8,128)S(1)} copy-done((f32[4,16,128]{2,1,0:T(8,128)S(1)}, f32[4,16,128]{2,1,0:T(8,128)}, u32[]{:S(2)}) %copy-start.4) | copy-done | bytes 32792
  7.3 0.0 copy-start.5
  7.3 0.8 %copy-done.5 = s32[1,1,8192]{2,1,0:T(1,128)S(1)} copy-done((s32[1,1,8192]{2,1,0:T(1,128)S(1)}, s32[1,1,8192]{2,1,0:T(1,128)}, u32[]{:S(2)}) %copy-start.5) | copy-done | bytes 32792
  8.0 0.0 copy-start.6
  8.0 0.7 %copy-done.6 = f32[6,2,5,5]{0,1,3,2:T(2,128)S(1)} copy-done((f32[6,2,5,5]{0,1,3,2:T(2,128)S(1)}, f32[6,2,5,5]{0,1,3,2:T(2,128)}, u32[]{:S(2)}) %copy-start.6) | copy-done | bytes 1224
  8.8 26.0 %shard_map.122 = (f32[10,4,16,128]{3,2,1,0:T(8,128)S(1)}, f32[12,2048]{1,0:T(8,128)S(1)}) custom-call(f32[10,4,16,128]{3,2,1,0:T(8,128)S(1)} %bitcast.8, f32[10,4,16,128]{3,2,1,0:T(8,128)S(1)} %bitcast.9, bf16[6,4,16,128]{3,2,1,0:T(8,128)(2,1)S(1)} %copy-done.3, f32[4,16,128]{2,1,0:T(8,128)S(1)} %copy-done.4, f32[5,5,2,6]{3,2,1,0:T(2,128)S(1)} %bitcast.12, ...), custom_call_target="tpu_custom_call" | custom-call | tf_op jit(solution)/shard_map/pallas_call | solution.py:539
  34.8 0.7 %copy.13 = f32[12,1,1,2048]{3,2,1,0:T(1,128)} copy(f32[12,1,1,2048]{3,0,2,1:T(8,128)S(1)} %bitcast.10) | data formatting | bytes 196608
  35.5 0.7 %copy.17 = f32[1,10,4,16,128]{4,3,2,1,0:T(8,128)} copy(f32[1,10,4,16,128]{4,3,2,1,0:T(8,128)S(1)} %bitcast.7) | data formatting | bytes 655360
Async XLA Ops:
  1.9 0.7 %copy-start.7 = (f32[3,10]{1,0:T(4,128)S(1)}, f32[3,10]{1,0:T(4,128)}, u32[]{:S(2)}) copy-start(f32[3,10]{1,0:T(4,128)} %metric_ref.1) | copy-start | bytes 364
  1.9 0.7 %copy-start.8 = (s32[1,1,64]{2,1,0:T(1,128)S(1)}, s32[1,1,64]{2,1,0:T(1,128)}, u32[]{:S(2)}) copy-start(s32[1,1,64]{2,1,0:T(1,128)} %param.20) | copy-start | bytes 772
  2.6 1.1 %copy-start = (bf16[12,3,4,16,128]{4,3,2,1,0:T(8,128)(2,1)S(1)}, bf16[12,3,4,16,128]{4,3,2,1,0:T(8,128)(2,1)}, u32[]{:S(2)}) copy-start(bf16[12,3,4,16,128]{4,3,2,1,0:T(8,128)(2,1)} %mode_in.1) | copy-start | bytes 1769476
  3.7 1.0 %copy-start.1 = (f32[1,10,4,16,128]{4,3,2,1,0:T(8,128)S(1)}, f32[1,10,4,16,128]{4,3,2,1,0:T(8,128)}, u32[]{:S(2)}) copy-start(f32[1,10,4,16,128]{4,3,2,1,0:T(8,128)} %param.11) | copy-start | bytes 983044
  4.6 1.0 %copy-start.2 = (f32[1,10,4,16,128]{4,3,2,1,0:T(8,128)S(1)}, f32[1,10,4,16,128]{4,3,2,1,0:T(8,128)}, u32[]{:S(2)}) copy-start(f32[1,10,4,16,128]{4,3,2,1,0:T(8,128)} %param.12) | copy-start | bytes 983044
  5.6 0.9 %copy-start.3 = (bf16[6,4,16,128]{3,2,1,0:T(8,128)(2,1)S(1)}, bf16[6,4,16,128]{3,2,1,0:T(8,128)(2,1)}, u32[]{:S(2)}) copy-start(bf16[6,4,16,128]{3,2,1,0:T(8,128)(2,1)} %face_in.1) | copy-start | bytes 294916
  6.5 0.8 %copy-start.4 = (f32[4,16,128]{2,1,0:T(8,128)S(1)}, f32[4,16,128]{2,1,0:T(8,128)}, u32[]{:S(2)}) copy-start(f32[4,16,128]{2,1,0:T(8,128)} %diag_in.1) | copy-start | bytes 98308
  7.3 0.8 %copy-start.5 = (s32[1,1,8192]{2,1,0:T(1,128)S(1)}, s32[1,1,8192]{2,1,0:T(1,128)}, u32[]{:S(2)}) copy-start(s32[1,1,8192]{2,1,0:T(1,128)} %param.21) | copy-start | bytes 98308
  8.0 0.7 %copy-start.6 = (f32[6,2,5,5]{0,1,3,2:T(2,128)S(1)}, f32[6,2,5,5]{0,1,3,2:T(2,128)}, u32[]{:S(2)}) copy-start(f32[6,2,5,5]{0,1,3,2:T(2,128)} %param.15) | copy-start | bytes 3604

commit v3 on v2

--- a/solution.py
+++ b/solution.py
@@ -487,7 +487,8 @@
         result = modes_owned[i, 0] * total[0:1]
         for d in range(1, 3):
             result = result + modes_owned[i, d] * total[d : d + 1]
-        sens_ref[:, i * TILE : (i + 1) * TILE] = result
+        for k in range(TILE // pitch):
+            sens_ref[:, i * (TILE // pitch) + k, :] = result[:, k * pitch : (k + 1) * pitch]
 
     for k in range(1, n_phase):
         phase_copy(k).wait_send()
@@ -540,7 +541,7 @@
         functools.partial(kernel, sizes),
         out_shape=(
             jax.ShapeDtypeStruct((comps, tile_a, tile_r, pitch), f32),
-            jax.ShapeDtypeStruct((count_k, owned), f32),
+            jax.ShapeDtypeStruct((count_k, owned // pitch, pitch), f32),
         ),
         in_specs=[hbm, hbm, hbm, hbm, hbm, smem, smem, hbm, smem, hbm, hbm],
         out_specs=(vmem, vmem),
@@ -581,7 +582,7 @@
             dma((n_phase,)),
         ],
         compiler_params=pltpu.CompilerParams(
-            collective_id=0, has_side_effects=True, vmem_limit_bytes=48 * 1024 * 1024
+            collective_id=0, has_side_effects=True, vmem_limit_bytes=60 * 1024 * 1024
         ),
     )(
         psi_start[0],

time: 36.7 us -> 31.1 us (0.85)
  local copies, waits for them, and re-layouts: 8.29 us -> 2.4 us
  Pallas kernels: 26 us -> 26.6 us
    unnamed x20 -> x4, local copies, waits for them, and re-layouts: 8.29 us -> 2.4 us
    pallas_call x1, Pallas kernels: 26 us -> 26.6 us  [body(): pl.pallas_call(functools.partial(kernel, sizes), out_shape=(jax.ShapeDtyp...]
where the time goes in v3:
time: 31.1 us; the launch traced here: 30.9 us
  Pallas kernels  26.6 us (86%)
  local copies, waits for them, and re-layouts  2.4 us (8%)
  between operations  1.94 us (6%)
    pallas_call x1, Pallas kernels, body(): pl.pallas_call(functools.partial(kernel, sizes), out_shape=(jax.ShapeDtyp...  26.6 us
    unnamed x4, local copies, waits for them, and re-layouts  2.4 us

profile of v3, /device:TPU:0, one launch (start us, length us, event | category | flops | bytes accessed | tf_op | source)
XLA Modules:
  0.0 30.9 jit_solution(16021947406684117969)
XLA Ops:
  1.9 26.6 %shard_map.122 = (f32[10,4,16,128]{3,2,1,0:T(8,128)}, f32[12,16,128]{2,1,0:T(8,128)}) custom-call(f32[10,4,16,128]{3,2,1,0:T(8,128)} %bitcast.8, f32[10,4,16,128]{3,2,1,0:T(8,128)} %bitcast.9, bf16[6,4,16,128]{3,2,1,0:T(8,128)(2,1)} %face_in.1, f32[4,16,128]{2,1,0:T(8,128)} %diag_in.1, f32[5,5,2,6]{3,2,1,0:T(2,128)} %bitcast.12, f32[1]{0:T(128)S(6)} %copy.17.omega_ref, ...), custom_call_target="tpu_custom_call" | custom-call | tf_op jit(solution)/shard_map/pallas_call | solution.py:540
  28.5 0.0 copy-start
  28.5 1.8 %copy.19 = f32[1,10,4,16,128]{4,3,2,1,0:T(8,128)} copy(f32[1,10,4,16,128]{4,3,2,1,0:T(8,128)} %bitcast.7) | data formatting | bytes 655360
  30.3 0.0 copy-done
  30.3 0.6 %copy.20 = f32[12,1,1,2048]{3,2,1,0:T(1,128)} copy(f32[12,1,1,2048]{3,2,1,0:T(1,128)S(1)} %bitcast.10) | data formatting | bytes 196608
Async XLA Ops:
  28.5 1.8 %copy-start = (f32[12,16,128]{2,1,0:T(8,128)S(1)}, f32[12,16,128]{2,1,0:T(8,128)}, u32[]{:S(2)}) copy-start(f32[12,16,128]{2,1,0:T(8,128)} %get-tuple-element.5) | copy-start | bytes 294916

commit v4 on v3

--- a/solution.py
+++ b/solution.py
@@ -59,6 +59,7 @@
     field_low,
     one_hot,
     row_mask,
+    sens,
     modes_owned,
     weighted,
     gathered,
@@ -124,42 +125,53 @@
         def _():
             pl.semaphore_signal(barrier, inc=1, device_id={name: me + 1}, device_id_type=MESH)
 
-    for flag, at, d in ((has_low[0], 0, 0), (has_high[0], tile_a + 1, 1)):
-        @pl.when(jnp.logical_not(flag))
-        def _():
-            coef[d, at] = jnp.zeros((tile_r, pitch), jnp.float32)
-            for s in range(ITERS):
-                for c in range(comps):
-                    psi[s, at, c, TOP : TOP + tile_r, :] = jnp.zeros(
-                        (tile_r, pitch), jnp.float32
-                    )
-
-    def axial_copy(s, up):
+    beyond = tile_a + 1 - jnp.where(ax > 0, 0, tile_a + 1)
+    coef[jnp.where(ax > 0, 1, 0), beyond] = jnp.zeros((tile_r, pitch), jnp.float32)
+    for s in range(ITERS):
+        for c in range(comps):
+            psi[s, beyond, c, TOP : TOP + tile_r, :] = jnp.zeros((tile_r, pitch), jnp.float32)
+
+    edge = jnp.where(ax > 0, 1, tile_a)
+    halo = jnp.where(ax > 0, 0, tile_a + 1)
+    first = jnp.where(ax > 0, 2, 1)
+
+    def layer(k):
+        return first + k if k < tile_a - 1 else edge
+
+    def half_rows(k):
+        return pl.ds(TOP + k * TOP, TOP)
+
+    def axial_copy(s, k, arriving=False):
         return pltpu.make_async_remote_copy(
-            src_ref=psi.at[s, tile_a if up else 1, :, rows, :],
-            dst_ref=psi.at[s, 0 if up else tile_a + 1, :, rows, :],
-            send_sem=send_sem.at[s, 0 if up else 1],
-            recv_sem=recv_sem.at[s, 0 if up else 1],
-            device_id={"axial": ax + 1 if up else ax - 1},
+            src_ref=psi.at[s, edge, :, half_rows(k), :],
+            dst_ref=psi.at[s, halo if arriving else tile_a + 1 - halo, :, half_rows(k), :],
+            send_sem=send_sem.at[s, k],
+            recv_sem=recv_sem.at[s, k],
+            device_id={"axial": 1 - ax},
             device_id_type=MESH,
         )
 
-    def radial_copy(s, up):
+    def radial_copy(s, up, part):
+        slots = pl.ds(0, tile_a - 1) if part == 0 else pl.ds(tile_a - 1, 1)
+        at = 2 + part * 2 + (0 if up else 1)
         return pltpu.make_async_remote_copy(
-            src_ref=radial_sent.at[s, 0 if up else 1],
-            dst_ref=(radial_low if up else radial_high).at[s],
-            send_sem=send_sem.at[s, 2 if up else 3],
-            recv_sem=recv_sem.at[s, 2 if up else 3],
+            src_ref=radial_sent.at[s, 0 if up else 1, slots],
+            dst_ref=(radial_low if up else radial_high).at[s, slots],
+            send_sem=send_sem.at[s, at],
+            recv_sem=recv_sem.at[s, at],
             device_id={"radial": rad + 1 if up else rad - 1},
             device_id_type=MESH,
         )
 
-    def face_copy(d):
+    leaving = jnp.where(ax > 0, 1, 0)
+    axial_face = 0
+
+    def face_copy(d, arriving=False):
         up = d % 2 == 0
         if d < 2:
-            src = coef.at[d, tile_a if up else 1]
-            dst = coef.at[d, 0 if up else tile_a + 1]
-            target = {"axial": ax + 1 if up else ax - 1}
+            src = coef.at[leaving, edge]
+            dst = coef.at[1 - leaving, halo] if arriving else coef.at[leaving, tile_a + 1 - halo]
+            target = {"axial": 1 - ax}
         else:
             src = face_sent.at[d - 2]
             dst = face_low if up else face_high
@@ -173,27 +185,25 @@
             device_id_type=MESH,
         )
 
-    def start_axial(s):
-        for up in (True, False):
-            @pl.when((has_high if up else has_low)[0])
-            def _():
-                axial_copy(s, up).start()
-
-    def start_radial(s):
-        for a in range(tile_a):
-            radial_sent[s, 0, :, a, :] = psi[s, a + 1, :, TOP + tile_r - 1, :]
-            radial_sent[s, 1, :, a, :] = psi[s, a + 1, :, TOP, :]
+    parts = (range(tile_a - 1), range(tile_a - 1, tile_a))
+
+    def start_radial(s, part):
+        for k in parts[part]:
+            radial_sent[s, 0, k] = psi[s, layer(k), :, TOP + tile_r - 1, :]
+            radial_sent[s, 1, k] = psi[s, layer(k), :, TOP, :]
         for up in (True, False):
             @pl.when((has_high if up else has_low)[1])
             def _():
-                radial_copy(s, up).start()
+                radial_copy(s, up, part).start()
 
     for copy in loads[:tile_a]:
         copy.wait()
     greeted = n_phase - 1 + sum(jnp.where(flag, 1, 0) for flag in has_low + has_high)
     pl.semaphore_wait(barrier, greeted)
-    start_axial(0)
-    start_radial(0)
+    for k in range(2):
+        axial_copy(0, k).start()
+    for part in range(2):
+        start_radial(0, part)
 
     loads[tile_a].wait()
     for a in range(tile_a):
@@ -202,8 +212,9 @@
     for a in range(tile_a):
         face_sent[0, a : a + 1, :] = coef[2, a + 1, tile_r - 1 : tile_r, :]
         face_sent[1, a : a + 1, :] = coef[3, a + 1, 0:1, :]
-    for d in range(4):
-        @pl.when((has_high if d % 2 == 0 else has_low)[d // 2])
+    face_copy(axial_face).start()
+    for d in (2, 3):
+        @pl.when((has_high if d == 2 else has_low)[1])
         def _():
             face_copy(d).start()
 
@@ -301,62 +312,79 @@
                 modes_owned[i, d, k : k + 6, :] = jnp.sum(picked, axis=1)
         return 0
 
-    def build(s, a, slot):
-        for c in range(comps):
-            own = psi[s, a, c, TOP : TOP + tile_r, :]
-            scaled = (
-                coef[0, a - 1] * psi[s, a - 1, c, TOP : TOP + tile_r, :],
-                coef[1, a + 1] * psi[s, a + 1, c, TOP : TOP + tile_r, :],
-                coef[2, a] * psi[s, a, c, TOP - 1 : TOP + tile_r - 1, :],
-                coef[3, a] * psi[s, a, c, TOP + 1 : TOP + tile_r + 1, :],
-                coef[4, a] * pltpu.roll(jnp.where(lane == pitch - 1, wrapped[c, a - 1], own), 1, 1),
-                coef[5, a]
-                * pltpu.roll(jnp.where(lane == 0, wrapped[c, a - 1], own), pitch - 1, 1),
-            )
-            for d in range(0, 6, 2):
-                at = (c * 6 + d) * TOP
-                for k in range(2):
-                    block = jnp.concatenate(
-                        [value[k * TOP : (k + 1) * TOP] for value in scaled[d : d + 2]], axis=0
-                    )
-                    high, low = split(block)
-                    columns = slice(k * pitch, (k + 1) * pitch)
+    low_lane = lane[:TOP]
+
+    def build(s, a, slot, halves):
+        for k in halves:
+            columns = slice(k * pitch, (k + 1) * pitch)
+            here = slice(k * TOP, (k + 1) * TOP)
+
+            def field(layer_at, c, shift):
+                at = TOP + k * TOP + shift
+                return psi[s, layer_at, c, at : at + TOP, :]
+
+            for c in range(comps):
+                own = field(a, c, 0)
+                wrap = wrapped[c, a - 1, here]
+                scaled = (
+                    coef[0, a - 1, here] * field(a - 1, c, 0),
+                    coef[1, a + 1, here] * field(a + 1, c, 0),
+                    coef[2, a, here] * field(a, c, -1),
+                    coef[3, a, here] * field(a, c, 1),
+                    coef[4, a, here] * pltpu.roll(jnp.where(low_lane == pitch - 1, wrap, own), 1, 1),
+                    coef[5, a, here]
+                    * pltpu.roll(jnp.where(low_lane == 0, wrap, own), pitch - 1, 1),
+                )
+                for d in range(0, 6, 2):
+                    at = (c * 6 + d) * TOP
+                    high, low = split(jnp.concatenate(scaled[d : d + 2], axis=0))
                     field_high[slot, at : at + 2 * TOP, columns] = high
                     field_low[slot, at : at + 2 * TOP, columns] = low
 
-    def update(s, a, slot):
-        both = jnp.dot(matrix[...], field_high[slot], preferred_element_type=jnp.float32)
-        rest = jnp.dot(matrix[:tall], field_low[slot], preferred_element_type=jnp.float32)
+    def update(s, a, slot, halves):
+        columns = slice(halves[0] * pitch, (halves[-1] + 1) * pitch)
+        both = jnp.dot(
+            matrix[...], field_high[slot, :, columns], preferred_element_type=jnp.float32
+        )
+        rest = jnp.dot(
+            matrix[:tall], field_low[slot, :, columns], preferred_element_type=jnp.float32
+        )
         total = both[:tall] + (both[tall:] + rest)
         omega = omega_ref[0]
-        scale = inverse[a - 1]
-
-        def incoming(c):
-            part = total[c * TOP : (c + 1) * TOP]
-            return jnp.concatenate([part[:, :pitch], part[:, pitch:]], axis=0)
-
-        for i in range(half):
-            real = psi[s, a, i, TOP : TOP + tile_r, :]
-            imag = psi[s, a, half + i, TOP : TOP + tile_r, :]
-            got_real = source_ref[i, a - 1] - omega * imag + incoming(i)
-            got_imag = source_ref[half + i, a - 1] + omega * real + incoming(half + i)
-            psi[s + 1, a, i, TOP : TOP + tile_r, :] = (1.0 - RELAX) * real + scale * got_real
-            psi[s + 1, a, half + i, TOP : TOP + tile_r, :] = (
-                1.0 - RELAX
-            ) * imag + scale * got_imag
-
-    def wait_axial(s):
+        for n, k in enumerate(halves):
+            here = slice(k * TOP, (k + 1) * TOP)
+            there = slice(TOP + k * TOP, 2 * TOP + k * TOP)
+            scale = inverse[a - 1, here]
+
+            def incoming(c):
+                return total[c * TOP : (c + 1) * TOP, n * pitch : (n + 1) * pitch]
+
+            for i in range(half):
+                real = psi[s, a, i, there, :]
+                imag = psi[s, a, half + i, there, :]
+                got_real = source_ref[i, a - 1, here] - omega * imag + incoming(i)
+                got_imag = source_ref[half + i, a - 1, here] + omega * real + incoming(half + i)
+                psi[s + 1, a, i, there, :] = (1.0 - RELAX) * real + scale * got_real
+                psi[s + 1, a, half + i, there, :] = (1.0 - RELAX) * imag + scale * got_imag
+
+    turned_sine = jnp.where(lane >= pitch // 2, sine, -sine)
+
+    def place_radial(s, part):
         for up in (True, False):
-            @pl.when((has_low if up else has_high)[0])
+            flag = (has_low if up else has_high)[1]
+            at = TOP - 1 if up else TOP + tile_r
+            got = radial_low if up else radial_high
+
+            @pl.when(flag)
             def _():
-                @pl.when(s == 0)
-                def _():
-                    face_copy(0 if up else 1).wait_recv()
-
-                axial_copy(s, up).wait_recv()
-
-    first = jnp.where(ax > 0, 2, 1)
-    turned_sine = jnp.where(lane >= pitch // 2, sine, -sine)
+                radial_copy(s, up, part).wait_recv()
+                for k in parts[part]:
+                    psi[s, layer(k), :, at, :] = got[s, k]
+
+            @pl.when(jnp.logical_not(flag))
+            def _():
+                for k in parts[part]:
+                    psi[s, layer(k), :, at, :] = jnp.zeros((comps, pitch), jnp.float32)
 
     def section(s, _):
         for c in range(comps):
@@ -373,28 +401,7 @@
             for copy in loads[tile_a + 4 :]:
                 copy.wait()
 
-        lax.fori_loop(
-            lax.div(n_tiles * s, ITERS), lax.div(n_tiles * (s + 1), ITERS), make_one_hot, 0
-        )
-        lax.fori_loop(
-            lax.div(own_tiles * s, ITERS), lax.div(own_tiles * (s + 1), ITERS), gather_modes, 0
-        )
-
-        for up in (True, False):
-            flag = (has_low if up else has_high)[1]
-            at = TOP - 1 if up else TOP + tile_r
-            got = radial_low if up else radial_high
-
-            @pl.when(flag)
-            def _():
-                radial_copy(s, up).wait_recv()
-                for a in range(tile_a):
-                    psi[s, a + 1, :, at, :] = got[s, :, a, :]
-
-            @pl.when(jnp.logical_not(flag))
-            def _():
-                for a in range(tile_a):
-                    psi[s, a + 1, :, at, :] = jnp.zeros((comps, pitch), jnp.float32)
+        place_radial(s, 0)
 
         @pl.when(s == 0)
         def _():
@@ -407,36 +414,63 @@
                     face_copy(d).wait_recv()
 
                 row = lax.broadcasted_iota(jnp.int32, (tile_r, pitch), 0)
-                edge = 0 if d == 2 else tile_r - 1
+                end = 0 if d == 2 else tile_r - 1
                 for a in range(tile_a):
                     moved = pltpu.roll(coef[d, a + 1], 1 if d == 2 else tile_r - 1, 0)
-                    coef[d, a + 1] = jnp.where(row == edge, 0.0, moved)
+                    coef[d, a + 1] = jnp.where(row == end, 0.0, moved)
 
                 @pl.when(flag)
                 def _():
                     for a in range(tile_a):
-                        coef[d, a + 1, edge : edge + 1, :] = got[a : a + 1, :]
-
-        if n_axial > 2:
-            wait_axial(s)
+                        coef[d, a + 1, end : end + 1, :] = got[a : a + 1, :]
+
         for k in range(tile_a - 1):
-            build(s, first + k, k)
+            build(s, layer(k), k, (0, 1))
         for k in range(tile_a - 1):
-            update(s, first + k, k)
-        if n_axial <= 2:
-            wait_axial(s)
-        last = jnp.where(ax > 0, 1, tile_a)
-        build(s, last, tile_a - 1)
-        update(s, last, tile_a - 1)
+            update(s, layer(k), k, (0, 1))
 
         @pl.when(s + 1 < ITERS)
         def _():
-            start_axial(s + 1)
-            start_radial(s + 1)
+            start_radial(s + 1, 0)
+
+        lax.fori_loop(
+            lax.div(n_tiles * s, ITERS), lax.div(n_tiles * (s + 1), ITERS), make_one_hot, 0
+        )
+        lax.fori_loop(
+            lax.div(own_tiles * s, 2 * ITERS),
+            lax.div(own_tiles * (s + 1), 2 * ITERS),
+            gather_modes,
+            0,
+        )
+        place_radial(s, 1)
+
+        @pl.when(s == 0)
+        def _():
+            face_copy(axial_face, arriving=True).wait_recv()
+
+        for k in range(2):
+            axial_copy(s, k, arriving=True).wait_recv()
+            build(s, edge, tile_a - 1, (k,))
+            update(s, edge, tile_a - 1, (k,))
+
+            @pl.when(s + 1 < ITERS)
+            def _():
+                axial_copy(s + 1, k).start()
+
+        @pl.when(s + 1 < ITERS)
+        def _():
+            start_radial(s + 1, 1)
 
         return 0
 
     lax.fori_loop(0, ITERS, section, 0)
+
+    results = [
+        pltpu.make_async_copy(psi.at[ITERS, a + 1, :, rows, :], out_ref.at[:, a], load_sem.at[a])
+        for a in range(tile_a)
+    ]
+    for copy in results:
+        copy.start()
 
     share = weight_ref[0]
     for a in range(tile_a):
@@ -474,8 +508,7 @@
         if k:
             phase_copy(k).start()
 
-    for a in range(tile_a):
-        out_ref[:, a] = psi[ITERS, a + 1, :, TOP : TOP + tile_r, :]
+    lax.fori_loop(own_tiles // 2, own_tiles, gather_modes, 0)
 
     for k in range(1, n_phase):
         phase_copy(k).wait_recv()
@@ -488,24 +521,39 @@
         for d in range(1, 3):
             result = result + modes_owned[i, d] * total[d : d + 1]
         for k in range(TILE // pitch):
-            sens_ref[:, i * (TILE // pitch) + k, :] = result[:, k * pitch : (k + 1) * pitch]
-
+            sens[:, i * (TILE // pitch) + k, :] = result[:, k * pitch : (k + 1) * pitch]
+
+    results.append(pltpu.make_async_copy(sens, sens_ref, load_sem.at[tile_a]))
+    results[-1].start()
     for k in range(1, n_phase):
         phase_copy(k).wait_send()
+    face_copy(axial_face).wait_send()
+    for s in range(ITERS):
+        for k in range(2):
+            axial_copy(s, k).wait_send()
     for up in (True, False):
-        flags = has_high if up else has_low
-
-        @pl.when(flags[0])
-        def _():
-            face_copy(0 if up else 1).wait_send()
-            for s in range(ITERS):
-                axial_copy(s, up).wait_send()
-
-        @pl.when(flags[1])
+        @pl.when((has_high if up else has_low)[1])
         def _():
             face_copy(2 if up else 3).wait_send()
             for s in range(ITERS):
-                radial_copy(s, up).wait_send()
+                for part in range(2):
+                    radial_copy(s, up, part).wait_send()
+
+    for copy in results:
+        copy.wait()
+
+
+def hand_on(psi_in, sens_in, psi_out, sens_out, sem):
+    copies = [pltpu.make_async_copy(sens_in, sens_out, sem.at[0])]
+    for c in range(0, psi_in.shape[0], 2):
+        own = pl.ds(c, 2)
+        copies.append(
+            pltpu.make_async_copy(psi_in.at[own], psi_out.at[own], sem.at[1 + c // 2])
+        )
+    for copy in copies:
+        copy.start()
+    for copy in copies:
+        copy.wait()
 
 
 def body(
@@ -532,7 +580,6 @@
     owned = cells // n_phase
     count_k = mode_shape.shape[0]
     f32, bf16 = jnp.float32, jnp.bfloat16
-    vmem = pl.BlockSpec(memory_space=pltpu.VMEM)
     smem = pl.BlockSpec(memory_space=pltpu.SMEM)
     hbm = pl.BlockSpec(memory_space=pltpu.HBM)
     dma = pltpu.SemaphoreType.DMA
@@ -544,7 +591,7 @@
             jax.ShapeDtypeStruct((count_k, owned // pitch, pitch), f32),
         ),
         in_specs=[hbm, hbm, hbm, hbm, hbm, smem, smem, hbm, smem, hbm, hbm],
-        out_specs=(vmem, vmem),
+        out_specs=(hbm, hbm),
         scratch_shapes=[
             pltpu.VMEM((ITERS + 1, tile_a + 2, comps, tile_r + 2 * TOP, pitch), f32),
             pltpu.VMEM((comps, tile_a, tile_r, pitch), f32),
@@ -554,9 +601,9 @@
             pltpu.VMEM((count_k, 3, tile_a, tile_r, pitch), bf16),
             pltpu.VMEM((1, nodes), jnp.int32),
             pltpu.VMEM((1, cells), jnp.int32),
-            pltpu.VMEM((ITERS, 2, comps, tile_a, pitch), f32),
-            pltpu.VMEM((ITERS, comps, tile_a, pitch), f32),
-            pltpu.VMEM((ITERS, comps, tile_a, pitch), f32),
+            pltpu.VMEM((ITERS, 2, tile_a, comps, pitch), f32),
+            pltpu.VMEM((ITERS, tile_a, comps, pitch), f32),
+            pltpu.VMEM((ITERS, tile_a, comps, pitch), f32),
             pltpu.VMEM((2, tile_a, pitch), f32),
             pltpu.VMEM((tile_a, pitch), f32),
             pltpu.VMEM((tile_a, pitch), f32),
@@ -569,13 +616,14 @@
             pltpu.VMEM((tile_a, depth, 2 * pitch), bf16),
             pltpu.VMEM((n_tiles, 2 * pitch, TILE), bf16),
             pltpu.VMEM((n_tiles, nodes // 2, TILE), f32),
+            pltpu.VMEM((count_k, owned // pitch, pitch), f32),
             pltpu.VMEM((own_tiles, 3, count_k, TILE), f32),
             pltpu.VMEM((3 * nodes, 2 * pitch), bf16),
             pltpu.VMEM((n_tiles, 3, TILE), f32),
             pltpu.VMEM((n_phase, own_tiles, 3, TILE), f32),
             dma((tile_a + 7,)),
-            dma((ITERS, 4)),
-            dma((ITERS, 4)),
+            dma((ITERS, 6)),
+            dma((ITERS, 6)),
             dma((4,)),
             dma((4,)),
             dma((n_phase,)),
@@ -597,11 +645,21 @@
         pairing[0],
         owner_order[0],
     )
+    results = (psi_out, sens)
+    psi_out, sens = pl.pallas_call(
+        hand_on,
+        out_shape=tuple(jax.ShapeDtypeStruct(value.shape, value.dtype) for value in results),
+        in_specs=[hbm, hbm],
+        out_specs=(hbm, hbm),
+        scratch_shapes=[dma((1 + comps // 2,))],
+        compiler_params=pltpu.CompilerParams(vmem_limit_bytes=60 * 1024 * 1024),
+    )(psi_out, sens)
     return (psi_out[None], sens.reshape(count_k, 1, 1, owned))
 
 
 def solution(mesh):
     sizes = tuple(mesh.shape[name] for name in ("phase", "axial", "radial"))
+    assert sizes[1] == 2
     return jax.shard_map(
         functools.partial(body, sizes),
         mesh=mesh,

time: 31.1 us -> 42.7 us (1.37)
  Pallas kernels: 26.6 us -> 40.6 us
  local copies, waits for them, and re-layouts: 2.4 us -> 0 us
    pallas_call x0 -> x1, Pallas kernels: none -> 14.1 us  [body(): pl.pallas_call(hand_on, out_shape=tuple((jax.ShapeDtypeStruct(value.shape...]
    unnamed x4 -> x0, local copies, waits for them, and re-layouts: 2.4 us -> none
where the time goes in v4:
time: 42.7 us; the launch traced here: 42.5 us
  Pallas kernels  40.6 us (95%)
  between operations  1.93 us (5%)
    pallas_call x1, Pallas kernels, body(): pl.pallas_call(functools.partial(kernel, sizes), out_shape=(jax.ShapeDtyp...  26.5 us
    pallas_call x1, Pallas kernels, body(): pl.pallas_call(hand_on, out_shape=tuple((jax.ShapeDtypeStruct(value.shape...  14.1 us

profile of v4, /device:TPU:0, one launch (start us, length us, event | category | flops | bytes accessed | tf_op | source)
XLA Modules:
  0.0 42.5 jit_solution(2886638278544280102)
XLA Ops:
  1.9 26.5 %shard_map.122 = (f32[10,4,16,128]{3,2,1,0:T(8,128)}, f32[12,16,128]{2,1,0:T(8,128)}) custom-call(f32[10,4,16,128]{3,2,1,0:T(8,128)} %bitcast.7, f32[10,4,16,128]{3,2,1,0:T(8,128)} %bitcast.8, bf16[6,4,16,128]{3,2,1,0:T(8,128)(2,1)} %face_in.1, f32[4,16,128]{2,1,0:T(8,128)} %diag_in.1, f32[5,5,2,6]{3,2,1,0:T(2,128)} %bitcast.10, f32[1]{0:T(128)S(6)} %copy.15.omega_ref, ...), custom_call_target="tpu_custom_call" | custom-call | tf_op jit(solution)/shard_map/pallas_call | solution.py:587
  28.5 14.1 %shard_map.123 = (f32[10,4,16,128]{3,2,1,0:T(8,128)}, f32[12,16,128]{2,1,0:T(8,128)}) custom-call(f32[10,4,16,128]{3,2,1,0:T(8,128)} %get-tuple-element.6.psi_in, f32[12,16,128]{2,1,0:T(8,128)} %get-tuple-element.7.sens_in), custom_call_target="tpu_custom_call" | custom-call | tf_op jit(solution)/shard_map/pallas_call | solution.py:649

commit v5 on v4

--- a/solution.py
+++ b/solution.py
@@ -196,28 +196,6 @@
             def _():
                 radial_copy(s, up, part).start()
 
-    for copy in loads[:tile_a]:
-        copy.wait()
-    greeted = n_phase - 1 + sum(jnp.where(flag, 1, 0) for flag in has_low + has_high)
-    pl.semaphore_wait(barrier, greeted)
-    for k in range(2):
-        axial_copy(0, k).start()
-    for part in range(2):
-        start_radial(0, part)
-
-    loads[tile_a].wait()
-    for a in range(tile_a):
-        for d in range(6):
-            coef[d, a + 1] = face_ref[d, a].astype(jnp.float32)
-    for a in range(tile_a):
-        face_sent[0, a : a + 1, :] = coef[2, a + 1, tile_r - 1 : tile_r, :]
-        face_sent[1, a : a + 1, :] = coef[3, a + 1, 0:1, :]
-    face_copy(axial_face).start()
-    for d in (2, 3):
-        @pl.when((has_high if d == 2 else has_low)[1])
-        def _():
-            face_copy(d).start()
-
     loads[tile_a + 1].wait()
     real = [flux_ref[j, :, 0, :] for j in range(half)]
     imag = [flux_ref[j, :, 1, :] for j in range(half)]
@@ -257,6 +235,36 @@
     partner = jnp.where(node >= nodes, node - nodes, node) == pairing_ref[...]
     pair_matrix[...] = jnp.where(partner, 1.0, 0.0).T.astype(jnp.bfloat16)
 
+    angle = 2.0 * math.pi / BLADES
+    turn = lax.rem(phase, BLADES)
+    cosine = jnp.float32(1.0)
+    sine = jnp.float32(0.0)
+    for k in range(1, BLADES):
+        cosine = jnp.where(turn == k, jnp.float32(math.cos(angle * k)), cosine)
+        sine = jnp.where(turn == k, jnp.float32(math.sin(angle * k)), sine)
+
+    for copy in loads[:tile_a]:
+        copy.wait()
+    greeted = n_phase - 1 + sum(jnp.where(flag, 1, 0) for flag in has_low + has_high)
+    pl.semaphore_wait(barrier, greeted)
+    for k in range(2):
+        axial_copy(0, k).start()
+    for part in range(2):
+        start_radial(0, part)
+
+    loads[tile_a].wait()
+    for a in range(tile_a):
+        for d in range(6):
+            coef[d, a + 1] = face_ref[d, a].astype(jnp.float32)
+    for a in range(tile_a):
+        face_sent[0, a : a + 1, :] = coef[2, a + 1, tile_r - 1 : tile_r, :]
+        face_sent[1, a : a + 1, :] = coef[3, a + 1, 0:1, :]
+    face_copy(axial_face).start()
+    for d in (2, 3):
+        @pl.when((has_high if d == 2 else has_low)[1])
+        def _():
+            face_copy(d).start()
+
     def permuted(value):
         stacked = jnp.concatenate(split(value), axis=0)
         return jnp.dot(pair_matrix[...], stacked, preferred_element_type=jnp.float32)
@@ -274,26 +282,22 @@
     for a in range(tile_a):
         inverse[a] = RELAX / diag_ref[a]
 
-    angle = 2.0 * math.pi / BLADES
-    turn = lax.rem(phase, BLADES)
-    cosine = jnp.float32(1.0)
-    sine = jnp.float32(0.0)
-    for k in range(1, BLADES):
-        cosine = jnp.where(turn == k, jnp.float32(math.cos(angle * k)), cosine)
-        sine = jnp.where(turn == k, jnp.float32(math.sin(angle * k)), sine)
-
-    def make_one_hot(u, _):
-        t = lax.rem(phase * own_tiles + u, n_tiles)
-        owner = owner_ref[:, pl.ds(pl.multiple_of(t * TILE, TILE), TILE)]
-        row = lax.div(owner, pitch)
-        column = owner - row * pitch
-        later = row >= fold
-        column = jnp.where(later, column + pitch, column)
-        row = jnp.where(later, row - fold, row)
-        at = lax.broadcasted_iota(jnp.int32, (2 * pitch, TILE), 0)
-        one_hot[t] = jnp.where(at == column, 1.0, 0.0).astype(jnp.bfloat16)
-        at = lax.broadcasted_iota(jnp.int32, (fold, TILE), 0)
-        row_mask[t] = jnp.where(at == row, 1.0, 0.0)
+    shift = pitch.bit_length() - 1
+
+    def make_one_hot(v, _):
+        for k in range(2):
+            t = lax.rem(phase * own_tiles + 2 * v + k, n_tiles)
+            owner = owner_ref[:, pl.ds(pl.multiple_of(t * TILE, TILE), TILE)]
+            row = owner >> shift
+            column = owner & (pitch - 1)
+            column = jnp.where(row >= fold, column + pitch, column)
+            row = row & (fold - 1)
+            at = lax.broadcasted_iota(jnp.int32, (2 * pitch, TILE), 0)
+            at, column = at.astype(jnp.bfloat16), column.astype(jnp.bfloat16)
+            one, zero = jnp.bfloat16(1.0), jnp.bfloat16(0.0)
+            one_hot[t] = jnp.where(at == column, one, zero)
+            at = lax.broadcasted_iota(jnp.int32, (fold, TILE), 0)
+            row_mask[t] = jnp.where(at == row, 1.0, 0.0)
         return 0
 
     def gather_modes(i, _):
@@ -434,7 +438,7 @@
             start_radial(s + 1, 0)
 
         lax.fori_loop(
-            lax.div(n_tiles * s, ITERS), lax.div(n_tiles * (s + 1), ITERS), make_one_hot, 0
+            lax.div(n_tiles * s, 2 * ITERS), lax.div(n_tiles * (s + 1), 2 * ITERS), make_one_hot, 0
         )
         lax.fori_loop(
             lax.div(own_tiles * s, 2 * ITERS),
@@ -543,16 +547,19 @@
         copy.wait()
 
 
-def hand_on(psi_in, sens_in, psi_out, sens_out, sem):
-    copies = [pltpu.make_async_copy(sens_in, sens_out, sem.at[0])]
+def hand_on(psi_in, sens_in, psi_out, sens_out, psi, sens, sem):
+    steps = [(sens_in, sens, sens_out)]
     for c in range(0, psi_in.shape[0], 2):
         own = pl.ds(c, 2)
-        copies.append(
-            pltpu.make_async_copy(psi_in.at[own], psi_out.at[own], sem.at[1 + c // 2])
-        )
-    for copy in copies:
+        steps.append((psi_in.at[own], psi.at[own], psi_out.at[own]))
+    arrive = [pltpu.make_async_copy(p, q, sem.at[0, k]) for k, (p, q, _) in enumerate(steps)]
+    leave = [pltpu.make_async_copy(q, r, sem.at[1, k]) for k, (_, q, r) in enumerate(steps)]
+    for copy in arrive:
         copy.start()
-    for copy in copies:
+    for k in range(len(steps)):
+        arrive[k].wait()
+        leave[k].start()
+    for copy in leave:
         copy.wait()
 
 
@@ -651,7 +658,8 @@
         out_shape=tuple(jax.ShapeDtypeStruct(value.shape, value.dtype) for value in results),
         in_specs=[hbm, hbm],
         out_specs=(hbm, hbm),
-        scratch_shapes=[dma((1 + comps // 2,))],
+        scratch_shapes=[pltpu.VMEM(value.shape, value.dtype) for value in results]
+        + [dma((2, 1 + comps // 2))],
         compiler_params=pltpu.CompilerParams(vmem_limit_bytes=60 * 1024 * 1024),
     )(psi_out, sens)
     return (psi_out[None], sens.reshape(count_k, 1, 1, owned))

time: 42.7 us -> 31.2 us (0.73)
  Pallas kernels: 40.6 us -> 29.1 us
    pallas_call x1, Pallas kernels: 14.1 us -> 1.75 us  [body(): pl.pallas_call(hand_on, out_shape=tuple((jax.ShapeDtypeStruct(value.shape...]
    pallas_call x1, Pallas kernels: 26.5 us -> 27.3 us  [body(): pl.pallas_call(functools.partial(kernel, sizes), out_shape=(jax.ShapeDtyp...]
where the time goes in v5:
time: 31.2 us; the launch traced here: 31 us
  Pallas kernels  29.1 us (93%)
  between operations  1.93 us (6%)
    pallas_call x1, Pallas kernels, body(): pl.pallas_call(functools.partial(kernel, sizes), out_shape=(jax.ShapeDtyp...  27.3 us
    pallas_call x1, Pallas kernels, body(): pl.pallas_call(hand_on, out_shape=tuple((jax.ShapeDtypeStruct(value.shape...  1.75 us

profile of v5, /device:TPU:0, one launch (start us, length us, event | category | flops | bytes accessed | tf_op | source)
XLA Modules:
  0.0 31.0 jit_solution(1359107015339795959)
XLA Ops:
  1.9 27.3 %shard_map.122 = (f32[10,4,16,128]{3,2,1,0:T(8,128)}, f32[12,16,128]{2,1,0:T(8,128)}) custom-call(f32[10,4,16,128]{3,2,1,0:T(8,128)} %bitcast.7, f32[10,4,16,128]{3,2,1,0:T(8,128)} %bitcast.8, bf16[6,4,16,128]{3,2,1,0:T(8,128)(2,1)} %face_in.1, f32[4,16,128]{2,1,0:T(8,128)} %diag_in.1, f32[5,5,2,6]{3,2,1,0:T(2,128)} %bitcast.10, f32[1]{0:T(128)S(6)} %copy.15.omega_ref, ...), custom_call_target="tpu_custom_call" | custom-call | tf_op jit(solution)/shard_map/pallas_call | solution.py:594
  29.3 1.7 %shard_map.123 = (f32[10,4,16,128]{3,2,1,0:T(8,128)}, f32[12,16,128]{2,1,0:T(8,128)}) custom-call(f32[10,4,16,128]{3,2,1,0:T(8,128)} %get-tuple-element.6.psi_in, f32[12,16,128]{2,1,0:T(8,128)} %get-tuple-element.7.sens_in), custom_call_target="tpu_custom_call" | custom-call | tf_op jit(solution)/shard_map/pallas_call | solution.py:656

commit v6 on v5

--- a/solution.py
+++ b/solution.py
@@ -141,9 +141,9 @@
     def half_rows(k):
         return pl.ds(TOP + k * TOP, TOP)
 
-    def axial_copy(s, k, arriving=False):
+    def axial_copy(s, k, arriving=False, source=None):
         return pltpu.make_async_remote_copy(
-            src_ref=psi.at[s, edge, :, half_rows(k), :],
+            src_ref=psi.at[s, edge, :, half_rows(k), :] if source is None else source,
             dst_ref=psi.at[s, halo if arriving else tile_a + 1 - halo, :, half_rows(k), :],
             send_sem=send_sem.at[s, k],
             recv_sem=recv_sem.at[s, k],
@@ -196,6 +196,28 @@
             def _():
                 radial_copy(s, up, part).start()
 
+    greeted = n_phase - 1 + sum(jnp.where(flag, 1, 0) for flag in has_low + has_high)
+    pl.semaphore_wait(barrier, greeted)
+    for k in range(2):
+        axial_copy(0, k, source=psi_in.at[:, edge - 1, pl.ds(k * TOP, TOP), :]).start()
+    for copy in loads[:tile_a]:
+        copy.wait()
+    for part in range(2):
+        start_radial(0, part)
+
+    loads[tile_a].wait()
+    for a in range(tile_a):
+        for d in range(6):
+            coef[d, a + 1] = face_ref[d, a].astype(jnp.float32)
+    for a in range(tile_a):
+        face_sent[0, a : a + 1, :] = coef[2, a + 1, tile_r - 1 : tile_r, :]
+        face_sent[1, a : a + 1, :] = coef[3, a + 1, 0:1, :]
+    face_copy(axial_face).start()
+    for d in (2, 3):
+        @pl.when((has_high if d == 2 else has_low)[1])
+        def _():
+            face_copy(d).start()
+
     loads[tile_a + 1].wait()
     real = [flux_ref[j, :, 0, :] for j in range(half)]
     imag = [flux_ref[j, :, 1, :] for j in range(half)]
@@ -242,28 +264,6 @@
     for k in range(1, BLADES):
         cosine = jnp.where(turn == k, jnp.float32(math.cos(angle * k)), cosine)
         sine = jnp.where(turn == k, jnp.float32(math.sin(angle * k)), sine)
-
-    for copy in loads[:tile_a]:
-        copy.wait()
-    greeted = n_phase - 1 + sum(jnp.where(flag, 1, 0) for flag in has_low + has_high)
-    pl.semaphore_wait(barrier, greeted)
-    for k in range(2):
-        axial_copy(0, k).start()
-    for part in range(2):
-        start_radial(0, part)
-
-    loads[tile_a].wait()
-    for a in range(tile_a):
-        for d in range(6):
-            coef[d, a + 1] = face_ref[d, a].astype(jnp.float32)
-    for a in range(tile_a):
-        face_sent[0, a : a + 1, :] = coef[2, a + 1, tile_r - 1 : tile_r, :]
-        face_sent[1, a : a + 1, :] = coef[3, a + 1, 0:1, :]
-    face_copy(axial_face).start()
-    for d in (2, 3):
-        @pl.when((has_high if d == 2 else has_low)[1])
-        def _():
-            face_copy(d).start()
 
     def permuted(value):
         stacked = jnp.concatenate(split(value), axis=0)
@@ -371,7 +371,8 @@
                 psi[s + 1, a, i, there, :] = (1.0 - RELAX) * real + scale * got_real
                 psi[s + 1, a, half + i, there, :] = (1.0 - RELAX) * imag + scale * got_imag
 
-    turned_sine = jnp.where(lane >= pitch // 2, sine, -sine)
+    face_lane = lax.broadcasted_iota(jnp.int32, (nodes, pitch), 1)
+    turned_sine = jnp.where(face_lane >= pitch // 2, sine, -sine)
 
     def place_radial(s, part):
         for up in (True, False):
@@ -391,14 +392,16 @@
                     psi[s, layer(k), :, at, :] = jnp.zeros((comps, pitch), jnp.float32)
 
     def section(s, _):
-        for c in range(comps):
-            whole = psi[s, 1 : tile_a + 1, c, TOP : TOP + tile_r, :].reshape(nodes, pitch)
-            wrapped[c] = permuted(whole).reshape(tile_a, tile_r, pitch)
-        for a in range(tile_a):
-            for j in range(half):
-                real, imag = wrapped[j, a], wrapped[half + j, a]
-                wrapped[j, a] = cosine * real - turned_sine * imag
-                wrapped[half + j, a] = turned_sine * real + cosine * imag
+        for j in range(half):
+            pair = [
+                psi[s, 1 : tile_a + 1, c, TOP : TOP + tile_r, :].reshape(nodes, pitch)
+                for c in (j, half + j)
+            ]
+            both = permuted(jnp.concatenate(pair, axis=1))
+            real, imag = both[:, :pitch], both[:, pitch:]
+            turned = (cosine * real - turned_sine * imag, turned_sine * real + cosine * imag)
+            for c, value in zip((j, half + j), turned):
+                wrapped[c] = value.reshape(tile_a, tile_r, pitch)
 
         @pl.when(s == 0)
         def _():
@@ -534,7 +537,8 @@
     face_copy(axial_face).wait_send()
     for s in range(ITERS):
         for k in range(2):
-            axial_copy(s, k).wait_send()
+            from_input = psi_in.at[:, edge - 1, pl.ds(k * TOP, TOP), :] if s == 0 else None
+            axial_copy(s, k, source=from_input).wait_send()
     for up in (True, False):
         @pl.when((has_high if up else has_low)[1])
         def _():

time: 31.2 us -> 30.1 us (0.965)
  Pallas kernels: 29.1 us -> 28 us
    pallas_call x1, Pallas kernels: 27.3 us -> 26.3 us  [body(): pl.pallas_call(functools.partial(kernel, sizes), out_shape=(jax.ShapeDtyp...]
where the time goes in v6:
time: 30.1 us; the launch traced here: 29.9 us
  Pallas kernels  28 us (93%)
  between operations  1.93 us (6%)
    pallas_call x1, Pallas kernels, body(): pl.pallas_call(functools.partial(kernel, sizes), out_shape=(jax.ShapeDtyp...  26.3 us
    pallas_call x1, Pallas kernels, body(): pl.pallas_call(hand_on, out_shape=tuple((jax.ShapeDtypeStruct(value.shape...  1.75 us

profile of v6, /device:TPU:0, one launch (start us, length us, event | category | flops | bytes accessed | tf_op | source)
XLA Modules:
  0.0 29.9 jit_solution(7832588709351803604)
XLA Ops:
  1.9 26.3 %shard_map.122 = (f32[10,4,16,128]{3,2,1,0:T(8,128)}, f32[12,16,128]{2,1,0:T(8,128)}) custom-call(f32[10,4,16,128]{3,2,1,0:T(8,128)} %bitcast.7, f32[10,4,16,128]{3,2,1,0:T(8,128)} %bitcast.8, bf16[6,4,16,128]{3,2,1,0:T(8,128)(2,1)} %face_in.1, f32[4,16,128]{2,1,0:T(8,128)} %diag_in.1, f32[5,5,2,6]{3,2,1,0:T(2,128)} %bitcast.10, f32[1]{0:T(128)S(6)} %copy.15.omega_ref, ...), custom_call_target="tpu_custom_call" | custom-call | tf_op jit(solution)/shard_map/pallas_call | solution.py:598
  28.2 1.7 %shard_map.123 = (f32[10,4,16,128]{3,2,1,0:T(8,128)}, f32[12,16,128]{2,1,0:T(8,128)}) custom-call(f32[10,4,16,128]{3,2,1,0:T(8,128)} %get-tuple-element.6.psi_in, f32[12,16,128]{2,1,0:T(8,128)} %get-tuple-element.7.sens_in), custom_call_target="tpu_custom_call" | custom-call | tf_op jit(solution)/shard_map/pallas_call | solution.py:660

commit v7 on v6

--- a/solution.py
+++ b/solution.py
@@ -457,11 +457,12 @@
 
         for k in range(2):
             axial_copy(s, k, arriving=True).wait_recv()
-            build(s, edge, tile_a - 1, (k,))
-            update(s, edge, tile_a - 1, (k,))
-
-            @pl.when(s + 1 < ITERS)
-            def _():
+        build(s, edge, tile_a - 1, (0, 1))
+        update(s, edge, tile_a - 1, (0, 1))
+
+        @pl.when(s + 1 < ITERS)
+        def _():
+            for k in range(2):
                 axial_copy(s + 1, k).start()
 
         @pl.when(s + 1 < ITERS)

time: 30.1 us -> 30.6 us (1.017)
  Pallas kernels: 28 us -> 28.4 us
    pallas_call x1, Pallas kernels: 26.3 us -> 26.7 us  [body(): pl.pallas_call(functools.partial(kernel, sizes), out_shape=(jax.ShapeDtyp...]
where the time goes in v7:
time: 30.6 us; the launch traced here: 30.4 us
  Pallas kernels  28.4 us (93%)
  between operations  1.93 us (6%)
    pallas_call x1, Pallas kernels, body(): pl.pallas_call(functools.partial(kernel, sizes), out_shape=(jax.ShapeDtyp...  26.7 us
    pallas_call x1, Pallas kernels, body(): pl.pallas_call(hand_on, out_shape=tuple((jax.ShapeDtypeStruct(value.shape...  1.75 us

profile of v7, /device:TPU:0, one launch (start us, length us, event | category | flops | bytes accessed | tf_op | source)
XLA Modules:
  0.0 30.4 jit_solution(9312544985015811300)
XLA Ops:
  1.9 26.7 %shard_map.122 = (f32[10,4,16,128]{3,2,1,0:T(8,128)}, f32[12,16,128]{2,1,0:T(8,128)}) custom-call(f32[10,4,16,128]{3,2,1,0:T(8,128)} %bitcast.7, f32[10,4,16,128]{3,2,1,0:T(8,128)} %bitcast.8, bf16[6,4,16,128]{3,2,1,0:T(8,128)(2,1)} %face_in.1, f32[4,16,128]{2,1,0:T(8,128)} %diag_in.1, f32[5,5,2,6]{3,2,1,0:T(2,128)} %bitcast.10, f32[1]{0:T(128)S(6)} %copy.15.omega_ref, ...), custom_call_target="tpu_custom_call" | custom-call | tf_op jit(solution)/shard_map/pallas_call | solution.py:599
  28.6 1.7 %shard_map.123 = (f32[10,4,16,128]{3,2,1,0:T(8,128)}, f32[12,16,128]{2,1,0:T(8,128)}) custom-call(f32[10,4,16,128]{3,2,1,0:T(8,128)} %get-tuple-element.6.psi_in, f32[12,16,128]{2,1,0:T(8,128)} %get-tuple-element.7.sens_in), custom_call_target="tpu_custom_call" | custom-call | tf_op jit(solution)/shard_map/pallas_call | solution.py:661
